TPU v7x, 32 devices: a whole 2x2x4 slice. The times are simulated.
32 devices in a mesh: row: 4 (over z), col: 8 (over y, x, core).
Axes of the slice: x: 2, y: 2, z: 4, core: 2. Of those that a mesh axis runs over, the one named last changes fastest.
Arguments:
- queries: bfloat16 [1024, 4096], P(('row', 'col')), may hold values from -8 to 8
- passages: bfloat16 [16384, 4096], P(('row', 'col')), may hold values from -8 to 8
- adapter: bfloat16 [4096, 768], replicated, may hold values from -0.09375 to 0.09375
- positives: int32 [1024], replicated, may hold values from 0 to 16383
Outputs:
- adapter_grad: float32 [4096, 768], P(('row', 'col'))
- query_grad: bfloat16 [1024, 4096], P(('row', 'col'))
- losses: float32 [1024], P(('row', 'col'))
All inputs are finite; a program needn't handle non-finite values.
Results may differ from a plain program's by a relative error of at most 0.0088.
Values may be sent and summed in bfloat16 or wider, within the bound.
A program may use at most 128 MiB of HBM per device.

v0:
```python
import jax
import jax.numpy as jnp
from jax import lax
from jax.sharding import PartitionSpec as P


def contract_first(left, right):
    return lax.dot_general(
        left, right, (((0,), (0,)), ((), ())), preferred_element_type=jnp.float32
    )


def per_device(queries, passages, adapter, positives):
    scale = adapter.shape[1] ** (-0.5)
    slab_rows = passages.shape[0]
    own_rows = queries.shape[0]
    here = lax.axis_index(("row", "col"))
    pa = jnp.dot(passages, adapter, preferred_element_type=jnp.float32).astype(jnp.bfloat16)
    local_qa = jnp.dot(queries, adapter, preferred_element_type=jnp.float32).astype(jnp.bfloat16)
    qa = lax.all_gather(local_qa, ("row", "col"), axis=0, tiled=True)
    scores = (
        lax.dot_general(qa, pa, (((1,), (1,)), ((), ())), preferred_element_type=jnp.float32)
        * scale
    )
    columns = here * slab_rows + jnp.arange(slab_rows, dtype=jnp.int32)
    hit = positives[:, None] == columns[None, :]
    local_max = jnp.max(scores, axis=1)
    local_pos = jnp.sum(jnp.where(hit, scores, 0.0), axis=1)
    top = lax.pmax(local_max, ("row", "col"))
    total, picked = lax.psum(
        (jnp.sum(jnp.exp(scores - top[:, None]), axis=1), local_pos), ("row", "col")
    )
    lse = top + jnp.log(total)
    probs = jnp.exp(scores - lse[:, None])
    dscores = ((probs - hit.astype(jnp.float32)) * scale).astype(jnp.bfloat16)
    dpa = contract_first(dscores, qa).astype(jnp.bfloat16)
    dqa_own = lax.psum_scatter(
        jnp.dot(dscores, pa, preferred_element_type=jnp.float32),
        ("row", "col"),
        scatter_dimension=0,
        tiled=True,
    ).astype(jnp.bfloat16)
    query_grad = lax.dot_general(
        dqa_own, adapter, (((1,), (1,)), ((), ())), preferred_element_type=jnp.float32
    ).astype(jnp.bfloat16)
    adapter_grad = lax.psum_scatter(
        contract_first(passages, dpa) + contract_first(queries, dqa_own),
        ("row", "col"),
        scatter_dimension=0,
        tiled=True,
    )
    first_row = here * own_rows
    losses = lax.dynamic_slice_in_dim(lse, first_row, own_rows, 0) - lax.dynamic_slice_in_dim(
        picked, first_row, own_rows, 0
    )
    return (adapter_grad, query_grad, losses)


def solution(mesh):
    placed = (P(("row", "col"), None), P(("row", "col"), None), P(), P())
    return jax.shard_map(
        per_device,
        mesh=mesh,
        in_specs=placed,
        out_specs=(P(("row", "col"), None), P(("row", "col"), None), P(("row", "col"))),
        check_vma=False,
    )
```

profile of v0, /device:TPU:0, one launch (start us, length us, event | category | flops | bytes accessed | tf_op | source)
XLA Modules:
  0.0 431.1 jit_solution(10524681862579875390)
XLA Ops:
  7.2 0.0 copy-start
  7.2 0.0 all-gather.2.cloned.1.call-start
  7.2 0.9 copy-done
  8.1 4.5 %convolution_convert_fusion.3 = bf16[32,768]{1,0:T(8,128)(2,1)} fusion(bf16[32,4096]{1,0:T(8,128)(2,1)S(1)} %copy-done, bf16[4096,768]{1,0:T(8,128)(2,1)} %param.6), kind=kOutput, calls=%fused_computation.12 | convolution fusion | flops 201351168 | bytes 6602752 | tf_op jit(solution)/shard_map/dot_general | solution.py:19
  12.7 0.0 all-gather.2.cloned.1.call-update
  12.7 0.0 reduce-scatter.3.cloned.1.call-start
  12.7 7.5 %convolution_convert_fusion.2 = bf16[512,768]{1,0:T(8,128)(2,1)S(1)} fusion(bf16[512,4096]{1,0:T(8,128)(2,1)} %param.5, bf16[4096,768]{1,0:T(8,128)(2,1)} %param.6), kind=kOutput, calls=%fused_computation.11 | convolution fusion | flops 3221618688 | bytes 11272192 | tf_op jit(solution)/shard_map/dot_general | solution.py:18
  20.2 0.0 copy-start.2
  20.2 50.2 %all-gather.2.cloned.1.call-done = bf16[1024,768]{1,0:T(8,128)(2,1)} async-done(((bf16[32,768]{1,0:T(8,128)(2,1)}), bf16[1024,768]{1,0:T(8,128)(2,1)}) %all-gather.2.cloned.1.call-update) | async-done | bytes 1572880 | tf_op jit(solution)/shard_map/all_gather | solution.py:20
  70.5 2.4 multiply_reduce_fusion
  72.9 38.9 %pmax.7 = f32[1024]{0:T(1024)S(1)} all-reduce(f32[1024]{0:T(1024)S(1)} %get-tuple-element.10), channel_id=1, replica_groups=mesh['row'=4,'col'=8] {'row','col'}, use_global_device_ids=true, to_apply=%region_1.2 | all-reduce | flops 1024 | bytes 8192 | tf_op jit(solution)/shard_map/pmax | solution.py:29
  111.8 0.0 copy-done.2
  111.8 0.6 fusion.3
  112.4 40.4 %all-reduce = (f32[1024]{0:T(1024)S(1)}, f32[1024]{0:T(1024)S(1)}) all-reduce(f32[1024]{0:T(1024)S(1)} %get-tuple-element.7, f32[1024]{0:T(1024)S(1)} %get-tuple-element.6), channel_id=1, replica_groups=mesh['row'=4,'col'=8] {'row','col'}, use_global_device_ids=true, to_apply=%region_3.4 | all-reduce | flops 2048 | bytes 16384 | tf_op jit(solution)/shard_map/psum | solution.py:30
  152.8 3.0 fusion.7
  155.8 0.0 reduce-scatter.3.cloned.1.call-update
  155.8 0.2 reduce-scatter.5.cloned.1.call-start
  156.1 12.4 %fusion.4 = f32[768,4096]{1,0:T(8,128)} fusion(bf16[512,4096]{1,0:T(8,128)(2,1)} %param.5, bf16[1024,768]{1,0:T(8,128)(2,1)} %all-gather.2.cloned.1.call-done, f32[1024,512]{0,1:T(8,128)S(1)} %get-tuple-element.11, s32[1024]{0:T(1024)S(1)} %copy-done.2, f32[1024]{0:T(1024)S(1)} %log_add_fusion, s32[512]{0:T(512)S(1)} %iota_add_fusion), kind=kOutput, calls=%fused_computation.13 | convolution fusion | flops 4030595072 | bytes 20457472 | tf_op jit(solution)/shard_map/dot_general | solution.py:8
  168.5 88.7 %reduce-scatter.3.cloned.1.call-done = f32[32,768]{1,0:T(8,128)} async-done(((f32[1024,768]{1,0:T(8,128)}), f32[32,768]{1,0:T(8,128)}) %reduce-scatter.3.cloned.1.call-update) | async-done | bytes 98320 | tf_op jit(solution)/shard_map/reduce_scatter | solution.py:37
  257.2 11.0 %add_bitcast_fusion = f32[4096,768]{0,1:T(8,128)} fusion(f32[768,4096]{1,0:T(8,128)} %fusion.4, bf16[32,4096]{1,0:T(8,128)(2,1)S(1)} %copy-done, f32[32,768]{1,0:T(8,128)} %reduce-scatter.3.cloned.1.call-done), kind=kOutput, calls=%fused_computation | convolution fusion | flops 204496896 | bytes 25526272 | tf_op jit(solution)/shard_map/dot_general | solution.py:8
  268.2 0.0 copy-start.1
  268.2 0.0 reduce-scatter.5.cloned.1.call-update
  268.2 0.6 dynamic-slice_subtract_fusion
  268.8 0.3 copy-done.1
  269.1 5.4 %convolution_convert_fusion = bf16[32,4096]{1,0:T(8,128)(2,1)} fusion(bf16[4096,768]{1,0:T(8,128)(2,1)} %param.6, f32[32,768]{1,0:T(8,128)S(1)} %copy-done.1), kind=kOutput, calls=%fused_computation.1 | convolution fusion | flops 201482240 | bytes 6651904 | tf_op jit(solution)/shard_map/dot_general | solution.py:43
  274.5 148.2 %reduce-scatter.5.cloned.1.call-done = f32[128,768]{0,1:T(8,128)} async-done(((f32[4096,768]{0,1:T(8,128)}), f32[128,768]{0,1:T(8,128)}) %reduce-scatter.5.cloned.1.call-update) | async-done | bytes 393232 | tf_op jit(solution)/shard_map/reduce_scatter | solution.py:46
  422.7 1.9 copy.7
  (2 shorter events, 0.0 us)
Async XLA Ops:
  7.2 1.0 copy-start
  7.2 63.3 %all-gather.2.cloned.1.call-start = ((), (), s32[]{:S(2)}) async-start(), calls=%async_computation.2 | async-start | bytes 1622016 | tf_op jit(solution)/shard_map/all_gather | solution.py:20
  12.7 244.5 %reduce-scatter.3.cloned.1.call-start = ((), (), s32[]{:S(2)}) async-start(), calls=%async_computation.3 | async-start | bytes 3244032 | tf_op jit(solution)/shard_map/reduce_scatter | solution.py:37
  20.2 91.6 %copy-start.2 = (s32[1024]{0:T(1024)S(1)}, s32[1024]{0:T(1024)}, u32[]{:S(2)}) copy-start(s32[1024]{0:T(1024)} %param.7) | copy-start | bytes 12292
  155.8 266.9 %reduce-scatter.5.cloned.1.call-start = ((), (), s32[]{:S(2)}) async-start(), calls=%async_computation.4 | async-start | bytes 12976128 | tf_op jit(solution)/shard_map/reduce_scatter | solution.py:46
  268.2 0.9 copy-start.1
Sparse Core Ops, SparseCore 0:
  12.8 57.6 all-gather.1
  155.9 101.1 reduce-scatter.2
  268.3 154.3 reduce-scatter.4
where the time goes:
time: 432 us; the launch traced here: 431 us
  waiting for transfers between devices  287 us (66%)
  blocking collectives  79.4 us (18%)
  matrix products  46.3 us (11%)
  between operations  13.8 us (3%)
    reduce_scatter x1, waiting for transfers between devices, per_device(): lax.psum_scatter(contract_first(passages, dpa) + contract_first(queries,...  148 us
    reduce_scatter x1, waiting for transfers between devices, per_device(): lax.psum_scatter(jnp.dot(dscores, pa, preferred_element_type=jnp.float32)...  88.7 us
    all_gather x1, waiting for transfers between devices, per_device(): qa = lax.all_gather(local_qa, ('row', 'col'), axis=0, tiled=True)  50.2 us
    psum x1, blocking collectives, per_device(): lax.psum((jnp.sum(jnp.exp(scores - top[:, None]), axis=1), local_pos), ('...  40.4 us
    pmax x1, blocking collectives, per_device(): top = lax.pmax(local_max, ('row', 'col'))  38.9 us
    dot_general x2, matrix products, contract_first(): lax.dot_general(left, right, (((0,), (0,)), ((), ())), preferred_element_...  23.5 us
  transfers between devices with their start and end apart: 3, of which 3 were waited for; matrix products, arithmetic and copies ran while one was open for 6% of the time, Pallas kernels for 0%

commit v1 on v0

v1 whole, which is shorter than its diff:
```python
import functools

import jax
import jax.numpy as jnp
from jax import lax
from jax.experimental import pallas as pl
from jax.experimental.pallas import tpu as pltpu
from jax.sharding import PartitionSpec as P

MESH = pl.DeviceIdType.MESH
LIMIT = 56 * 1024 * 1024


class Grid:
    def __init__(self, n_row, n_col):
        factors, left = [], n_col
        while left % 2 == 0:
            factors.append(2)
            left //= 2
        if left > 1:
            factors.insert(0, left)
        self.sizes = [n_row] + factors[::-1] if left == 1 else [n_row] + factors
        self.n_row, self.n_col = n_row, n_col
        self.core = len(self.sizes) - 1
        self.strides = [0] * len(self.sizes)
        stride = 1
        for dim in range(self.core, 0, -1):
            self.strides[dim] = stride
            stride *= self.sizes[dim]

    def place(self):
        row, col = lax.axis_index("row"), lax.axis_index("col")
        mine = [row]
        for dim in range(1, self.core + 1):
            mine.append(lax.rem(col // self.strides[dim], self.sizes[dim]))
        return row, col, mine

    def partner(self, row, col, mine, dim, value):
        if dim == 0:
            return (value, col)
        return (row, col + (value - mine[dim]) * self.strides[dim])

    def moved(self, mine, dim, offset):
        size = self.sizes[dim]
        return lax.rem(mine[dim] + offset + size, size)

    def middle(self, first):
        dims = list(range(1, self.core))
        first = first % max(len(dims), 1)
        return dims[first:] + dims[:first]


def greet(grid, row, col, mine):
    barrier = pltpu.get_barrier_semaphore()
    count = 0
    for dim, size in enumerate(grid.sizes):
        for offset in range(1, size):
            pl.semaphore_signal(
                barrier,
                inc=1,
                device_id=grid.partner(row, col, mine, dim, grid.moved(mine, dim, offset)),
                device_id_type=MESH,
            )
            count += 1
    pl.semaphore_wait(barrier, count)


def semaphore_table(grid, orders):
    table, count = {}, 0
    for part, (_, _, order) in enumerate(orders):
        for dim in order:
            for offset in range(1, grid.sizes[dim]):
                table[part, dim, offset] = count
                count += 1
    return table, count


def gather_kernel(grid, orders, table, x_ref, o_ref, send_sem, recv_sem):
    row, col, mine = grid.place()
    greet(grid, row, col, mine)
    o_ref[tuple(mine)] = x_ref[...]
    started = []

    def region(part, step, values):
        first, last, order = orders[part]
        done = order[:step]
        return o_ref.at[
            tuple(slice(None) if d in done else values[d] for d in range(len(values)))
            + (pl.ds(first, last - first),)
        ]

    def start(part, step):
        dim = orders[part][2][step]
        source = region(part, step, mine)
        for offset in range(1, grid.sizes[dim]):
            sem = table[part, dim, offset]
            copy = pltpu.make_async_remote_copy(
                src_ref=source,
                dst_ref=source,
                send_sem=send_sem.at[sem],
                recv_sem=recv_sem.at[sem],
                device_id=grid.partner(row, col, mine, dim, grid.moved(mine, dim, offset)),
                device_id_type=MESH,
            )
            copy.start()
            started.append(copy)

    def finish(part, step):
        dim = orders[part][2][step]
        for offset in range(1, grid.sizes[dim]):
            sem = table[part, dim, offset]
            theirs = list(mine)
            theirs[dim] = grid.moved(mine, dim, -offset)
            landing = region(part, step, theirs)
            pltpu.make_async_remote_copy(
                src_ref=landing,
                dst_ref=landing,
                send_sem=send_sem.at[sem],
                recv_sem=recv_sem.at[sem],
                device_id=grid.partner(row, col, mine, dim, theirs[dim]),
                device_id_type=MESH,
            ).wait_recv()

    for part in range(len(orders)):
        start(part, 0)
    steps = len(grid.sizes)
    for step in range(steps):
        for part in range(len(orders)):
            finish(part, step)
            if step + 1 < steps:
                start(part, step + 1)
    for copy in started:
        copy.wait_send()


def gather(grid, x, cuts, collective_id):
    rows, cols = x.shape
    orders = []
    for part, (first, last) in enumerate(zip(cuts[:-1], cuts[1:])):
        orders.append((first, last, [0] + grid.middle(part) + [grid.core]))
    table, count = semaphore_table(grid, orders)
    out = pl.pallas_call(
        functools.partial(gather_kernel, grid, orders, table),
        out_shape=jax.ShapeDtypeStruct(tuple(grid.sizes) + (rows, cols), x.dtype),
        in_specs=[pl.BlockSpec(memory_space=pltpu.VMEM)],
        out_specs=pl.BlockSpec(memory_space=pltpu.VMEM),
        scratch_shapes=[pltpu.SemaphoreType.DMA((count,)), pltpu.SemaphoreType.DMA((count,))],
        compiler_params=pltpu.CompilerParams(
            collective_id=collective_id, has_side_effects=True, vmem_limit_bytes=LIMIT
        ),
    )(x)
    return out.reshape(grid.n_row * grid.n_col, rows, cols)


def reduce_kernel(grid, orders, table, produce, n_in, *refs):
    ins, out_ref = refs[:n_in], refs[n_in]
    total, core_out, core_in = refs[n_in + 1 : n_in + 4]
    core_send, core_recv, send_sem, recv_sem = refs[n_in + 4 : n_in + 8]
    n_parts = len(orders)
    outgoing = refs[n_in + 8 : n_in + 8 + len(table)]
    incoming = refs[n_in + 8 + len(table) :]
    row, col, mine = grid.place()
    greet(grid, row, col, mine)
    core = grid.core
    other = 1 - mine[core]
    between = (slice(None),) * (core - 1)
    shape = total.shape[1:]
    core_copies = []
    for z in range(grid.n_row):
        total[z] = produce(z, *ins).reshape(shape)
        core_out[z] = total[(z,) + between + (other,)].astype(jnp.bfloat16)
        copy = pltpu.make_async_remote_copy(
            src_ref=core_out.at[z],
            dst_ref=core_in.at[z],
            send_sem=core_send.at[z],
            recv_sem=core_recv.at[z],
            device_id=grid.partner(row, col, mine, core, other),
            device_id_type=MESH,
        )
        copy.start()
        core_copies.append(copy)
    for z, copy in enumerate(core_copies):
        copy.wait_recv()
        where = (z,) + between + (mine[core],)
        total[where] = total[where] + core_in[z].astype(jnp.float32)

    started = []

    def region(part, step, value):
        first, last, order = orders[part]
        dim, done = order[step], order[:step]
        index = []
        for d in range(core):
            index.append(value if d == dim else mine[d] if d in done else slice(None))
        return tuple(index) + (mine[core], pl.ds(first, last - first))

    def start(part, step):
        dim = orders[part][2][step]
        for offset in range(1, grid.sizes[dim]):
            sem = table[part, dim, offset]
            value = grid.moved(mine, dim, offset)
            outgoing[sem][...] = total[region(part, step, value)].astype(jnp.bfloat16)
            copy = pltpu.make_async_remote_copy(
                src_ref=outgoing[sem],
                dst_ref=incoming[sem],
                send_sem=send_sem.at[sem],
                recv_sem=recv_sem.at[sem],
                device_id=grid.partner(row, col, mine, dim, value),
                device_id_type=MESH,
            )
            copy.start()
            started.append(copy)
            waiting[part, step, offset] = copy

    def finish(part, step):
        dim = orders[part][2][step]
        where = region(part, step, mine[dim])
        value = total[where]
        for offset in range(1, grid.sizes[dim]):
            waiting[part, step, offset].wait_recv()
            value = value + incoming[table[part, dim, offset]][...].astype(jnp.float32)
        total[where] = value

    waiting = {}
    for part in range(n_parts):
        start(part, 0)
    steps = core
    turns = []
    for part in range(n_parts):
        late = 1.5 if orders[part][2][0] == 0 else 0
        for step in range(steps):
            turns.append((step + late, part, step))
    for _, part, step in sorted(turns):
        finish(part, step)
        if step + 1 < steps:
            start(part, step + 1)
    out_ref[...] = total[tuple(mine)]
    for copy in core_copies + started:
        copy.wait_send()


def reduce_scatter(grid, produce, ins, rows, cols, plan, collective_id):
    core = grid.core
    orders = []
    for first, last, turn, row_first in plan:
        middle = grid.middle(turn)
        orders.append((first, last, [0] + middle if row_first else middle + [0]))
    table, count = semaphore_table(grid, orders)
    buffers = []
    for part, (first, last, order) in enumerate(orders):
        for step, dim in enumerate(order):
            left = tuple(grid.sizes[d] for d in range(core) if d not in order[: step + 1])
            for offset in range(1, grid.sizes[dim]):
                buffers.append(pltpu.VMEM(left + (last - first, cols), jnp.bfloat16))
    sizes = tuple(grid.sizes)
    half = pltpu.VMEM(sizes[:-1] + (rows, cols), jnp.bfloat16)
    return pl.pallas_call(
        functools.partial(reduce_kernel, grid, orders, table, produce, len(ins)),
        out_shape=jax.ShapeDtypeStruct((rows, cols), jnp.float32),
        in_specs=[pl.BlockSpec(memory_space=pltpu.VMEM)] * len(ins),
        out_specs=pl.BlockSpec(memory_space=pltpu.VMEM),
        scratch_shapes=[
            pltpu.VMEM(sizes + (rows, cols), jnp.float32),
            half,
            half,
            pltpu.SemaphoreType.DMA((grid.n_row,)),
            pltpu.SemaphoreType.DMA((grid.n_row,)),
            pltpu.SemaphoreType.DMA((count,)),
            pltpu.SemaphoreType.DMA((count,)),
        ]
        + buffers
        + buffers,
        compiler_params=pltpu.CompilerParams(
            collective_id=collective_id, has_side_effects=True, vmem_limit_bytes=LIMIT
        ),
    )(*ins)


def contract_first(left, right):
    return lax.dot_general(
        left, right, (((0,), (0,)), ((), ())), preferred_element_type=jnp.float32
    )


def query_slab(z, height, dscores_ref, pa_ref):
    return jnp.dot(
        dscores_ref[z * height : (z + 1) * height, :],
        pa_ref[...],
        preferred_element_type=jnp.float32,
    )


def adapter_slab(z, width, passages_ref, dpa_ref, queries_ref, dqa_ref):
    columns = slice(z * width, (z + 1) * width)
    return contract_first(passages_ref[:, columns], dpa_ref[...]) + contract_first(
        queries_ref[:, columns], dqa_ref[...]
    )


def thirds(rows):
    unit = rows // 16
    large = (unit * 3) // 8
    if large == 0:
        half = (unit // 2) * 16
        if half == 0:
            return [(0, rows, 0, False)]
        return [(0, half, 0, False), (half, rows, 1, False)]
    return [
        (0, 16 * large, 0, False),
        (16 * large, 32 * large, 1, False),
        (32 * large, rows, 0, True),
    ]


def per_device(grid, queries, passages, adapter, positives):
    scale = adapter.shape[1] ** (-0.5)
    slab_rows = passages.shape[0]
    own_rows, width = queries.shape
    emb = adapter.shape[1]
    n = grid.n_row * grid.n_col
    n_query = own_rows * n
    here = lax.axis_index(("row", "col"))
    local_qa = jnp.dot(queries, adapter, preferred_element_type=jnp.float32).astype(jnp.bfloat16)
    pa = jnp.dot(passages, adapter, preferred_element_type=jnp.float32).astype(jnp.bfloat16)
    cuts = [0, own_rows // 2, own_rows] if own_rows % 32 == 0 else [0, own_rows]
    qa = gather(grid, local_qa, cuts, 0).reshape(n_query, emb)
    scores = (
        lax.dot_general(qa, pa, (((1,), (1,)), ((), ())), preferred_element_type=jnp.float32)
        * scale
    )
    columns = here * slab_rows + jnp.arange(slab_rows, dtype=jnp.int32)
    hit = positives[:, None] == columns[None, :]
    local_max = jnp.max(scores, axis=1)
    local_pos = jnp.sum(jnp.where(hit, scores, 0.0), axis=1)
    local_sum = jnp.sum(jnp.exp(scores - local_max[:, None]), axis=1)
    stats = jnp.stack([local_max, local_sum, local_pos]).reshape(-1, 128)
    stats = gather(grid, stats, [0, 8, stats.shape[0]], 1).reshape(n, 3, n_query)
    top = jnp.max(stats[:, 0], axis=0)
    total = jnp.sum(stats[:, 1] * jnp.exp(stats[:, 0] - top), axis=0)
    picked = jnp.sum(stats[:, 2], axis=0)
    lse = top + jnp.log(total)
    probs = jnp.exp(scores - lse[:, None])
    dscores = ((probs - hit.astype(jnp.float32)) * scale).astype(jnp.bfloat16)
    dqa_own = reduce_scatter(
        grid,
        lambda z, *refs: query_slab(z, n_query // grid.n_row, *refs),
        (dscores, pa),
        own_rows,
        emb,
        thirds(own_rows),
        2,
    ).astype(jnp.bfloat16)
    dpa = contract_first(dscores, qa).astype(jnp.bfloat16)
    query_grad = lax.dot_general(
        dqa_own, adapter, (((1,), (1,)), ((), ())), preferred_element_type=jnp.float32
    ).astype(jnp.bfloat16)
    adapter_grad = reduce_scatter(
        grid,
        lambda z, *refs: adapter_slab(z, width // grid.n_row, *refs),
        (passages, dpa, queries, dqa_own),
        width // n,
        emb,
        thirds(width // n),
        3,
    )
    first_row = here * own_rows
    losses = lax.dynamic_slice_in_dim(lse - picked, first_row, own_rows, 0)
    return (adapter_grad, query_grad, losses)


def solution(mesh):
    grid = Grid(mesh.shape["row"], mesh.shape["col"])
    placed = (P(("row", "col"), None), P(("row", "col"), None), P(), P())
    return jax.shard_map(
        functools.partial(per_device, grid),
        mesh=mesh,
        in_specs=placed,
        out_specs=(P(("row", "col"), None), P(("row", "col"), None), P(("row", "col"))),
        check_vma=False,
    )
```

time: 432 us -> 145 us (0.34)
  waiting for transfers between devices: 287 us -> 0 us
  Pallas kernels: 0 us -> 119 us
  blocking collectives: 79.4 us -> 0 us
  matrix products: 46.3 us -> 17.5 us
  between operations: 13.8 us -> 0.79 us
    reduce_scatter x2 -> x0, waiting for transfers between devices: 237 us -> none  [the longest x1 148 us: per_device(): lax.psum_scatter(contract_first(passages, dpa) + contract_first(queries,...]
    pallas_call x0 -> x4, Pallas kernels: none -> 119 us  [the longest x2 81.4 us: reduce_scatter(): pl.pallas_call(functools.partial(reduce_kernel, grid, orders, table, prod...]
    all_gather x1 -> x0, waiting for transfers between devices: 50.2 us -> none  [per_device(): qa = lax.all_gather(local_qa, ('row', 'col'), axis=0, tiled=True)]
    psum x1 -> x0, blocking collectives: 40.4 us -> none  [per_device(): lax.psum((jnp.sum(jnp.exp(scores - top[:, None]), axis=1), local_pos), ('...]
    pmax x1 -> x0, blocking collectives: 38.9 us -> none  [per_device(): top = lax.pmax(local_max, ('row', 'col'))]
    dot_general x2 -> x1, matrix products: 23.5 us -> 1.94 us  [contract_first(): lax.dot_general(left, right, (((0,), (0,)), ((), ())), preferred_element_...]
  transfers between devices with their start and end apart: 3 -> 0, of which waited for: 3 -> 0; matrix products, arithmetic and copies ran while one was open for 6% -> 0% of each run, Pallas kernels for 0% -> 0%
where the time goes in v1:
time: 145 us
  Pallas kernels  119 us (82%)
  matrix products  17.5 us (12%)
  local copies, waits for them, and re-layouts  3.47 us (2%)
  other arithmetic  3.45 us (2%)
    pallas_call x2, Pallas kernels, reduce_scatter(): pl.pallas_call(functools.partial(reduce_kernel, grid, orders, table, prod...  81.4 us
    pallas_call x2, Pallas kernels, gather(): pl.pallas_call(functools.partial(gather_kernel, grid, orders, table), out...  38 us
    dot_general x1, matrix products, per_device(): jnp.dot(passages, adapter, preferred_element_type=jnp.float32)  5.63 us
    dot_general x1, matrix products, per_device(): jnp.dot(queries, adapter, preferred_element_type=jnp.float32)  4.76 us

profile of v1, /device:TPU:0, one launch (start us, length us, event | category | flops | bytes accessed | tf_op | source)
XLA Modules:
  0.0 144.6 jit_solution(1879558053522484569)
XLA Ops:
  0.6 0.0 copy-start
  0.7 4.8 %convolution_convert_fusion.3.x_ref = bf16[32,768]{1,0:T(8,128)(2,1)} fusion(bf16[32,4096]{1,0:T(8,128)(2,1)} %refs_2_.1, bf16[4096,768]{1,0:T(8,128)(2,1)} %param.6), kind=kOutput, calls=%fused_computation.11 | convolution fusion | flops 201351168 | bytes 6602752 | tf_op jit(solution)/shard_map/dot_general | solution.py:323
  5.4 0.0 copy-done
  5.4 5.6 %convolution_convert_fusion.2.refs_1_ = bf16[512,768]{1,0:T(8,128)(2,1)S(1)} fusion(bf16[512,4096]{1,0:T(8,128)(2,1)} %refs_0_.1, bf16[4096,768]{1,0:T(8,128)(2,1)S(1)} %copy-done), kind=kOutput, calls=%fused_computation.10 | convolution fusion | flops 3221618688 | bytes 11272192 | tf_op jit(solution)/shard_map/dot_general | solution.py:324
  11.1 0.0 copy-start.4
  11.1 23.9 %shard_map.67 = bf16[4,2,2,2,32,768]{5,4,3,2,1,0:T(8,128)(2,1)} custom-call(bf16[32,768]{1,0:T(8,128)(2,1)} %convolution_convert_fusion.3.x_ref), custom_call_target="tpu_custom_call" | custom-call | tf_op jit(solution)/shard_map/pallas_call | solution.py:142
  35.0 0.0 copy-start.6
  35.0 2.5 %multiply_reduce_fusion = (f32[1024]{0:T(1024)S(1)}, f32[1024,512]{1,0:T(8,128)S(1)}) fusion(bf16[1024,768]{1,0:T(8,128)(2,1)} %bitcast.30, bf16[512,768]{1,0:T(8,128)(2,1)S(1)} %convolution_convert_fusion.2.refs_1_), kind=kOutput, calls=%fused_computation.8 | convolution fusion | flops 806353920 | bytes 4460544 | tf_op jit(solution)/shard_map/dot_general | solution.py:328
  37.5 0.0 copy-done.4
  37.5 0.0 copy-done.6
  37.5 0.9 exponential_reduce_fusion
  38.4 0.6 reshape.22.x_ref
  39.0 14.1 %shard_map.68 = f32[4,2,2,2,24,128]{5,4,3,2,1,0:T(8,128)} custom-call(f32[24,128]{1,0:T(8,128)} %reshape.22.x_ref), custom_call_target="tpu_custom_call" | custom-call | tf_op jit(solution)/shard_map/pallas_call | solution.py:142
  53.1 1.1 reshape_reshape.7
  54.3 0.0 copy-start.2
  54.3 0.3 slice_reduce_fusion
  54.6 0.1 fusion.7
  54.7 0.6 fusion.3.refs_0_
  55.3 0.3 copy-done.2
  55.7 0.0 copy-start.1
  55.7 0.0 slice-start
  55.7 1.9 %convolution_convert_fusion.1.refs_1_ = bf16[512,768]{1,0:T(8,128)(2,1)} fusion(bf16[1024,512]{1,0:T(8,128)(2,1)S(1)} %fusion.3.refs_0_, bf16[1024,768]{1,0:T(8,128)(2,1)S(1)} %bitcast.31), kind=kOutput, calls=%fused_computation.9 | convolution fusion | flops 805699584 | bytes 3407872 | tf_op jit(solution)/shard_map/dot_general | solution.py:280
  57.6 0.0 copy-done.1
  57.6 0.0 slice-start.1
  57.6 23.9 %shard_map.69 = f32[32,768]{1,0:T(8,128)} custom-call(bf16[1024,512]{1,0:T(8,128)(2,1)} %copy-done.1, bf16[512,768]{1,0:T(8,128)(2,1)} %copy-done.4), custom_call_target="tpu_custom_call" | custom-call | tf_op jit(solution)/shard_map/pallas_call | solution.py:257
  81.5 1.5 %convert_element_type.26.refs_3_ = bf16[32,768]{1,0:T(8,128)(2,1)} convert(f32[32,768]{1,0:T(8,128)} %shard_map.69) | non-fusion elementwise | flops 24576 | bytes 147456 | tf_op jit(solution)/shard_map/convert_element_type | solution.py:352
  83.1 0.0 copy-start.5
  83.1 57.5 %shard_map.70 = f32[128,768]{1,0:T(8,128)} custom-call(bf16[512,4096]{1,0:T(8,128)(2,1)} %refs_0_.1, bf16[512,768]{1,0:T(8,128)(2,1)} %convolution_convert_fusion.1.refs_1_, bf16[32,4096]{1,0:T(8,128)(2,1)} %refs_2_.1, bf16[32,768]{1,0:T(8,128)(2,1)} %convert_element_type.26.refs_3_), custom_call_target="tpu_custom_call" | custom-call | tf_op jit(solution)/shard_map/pallas_call | solution.py:257
  140.6 0.6 dynamic_slice.3
  141.2 0.0 slice-done
  141.2 0.0 slice-done.1
  141.2 0.0 copy-done.5
  141.2 0.0 copy-start.3
  141.2 2.6 %convolution_convert_fusion = bf16[32,4096]{1,0:T(8,128)(2,1)} fusion(bf16[32,768]{1,0:T(8,128)(2,1)S(1)} %copy-done.5, bf16[4096,768]{1,0:T(8,128)(2,1)S(1)} %bitcast.29), kind=kOutput, calls=%fused_computation | convolution fusion | flops 201457664 | bytes 6602752 | tf_op jit(solution)/shard_map/dot_general | solution.py:354
  143.8 0.0 copy-done.3
  143.8 0.7 copy.26
  (4 shorter events, 0.0 us)
Async XLA Ops:
  0.6 4.8 %copy-start = (bf16[4096,768]{1,0:T(8,128)(2,1)S(1)}, bf16[4096,768]{1,0:T(8,128)(2,1)}, u32[]{:S(2)}) copy-start(bf16[4096,768]{1,0:T(8,128)(2,1)} %param.6) | copy-start | bytes 18874372
  11.1 26.5 %copy-start.4 = (bf16[512,768]{1,0:T(8,128)(2,1)}, bf16[512,768]{1,0:T(8,128)(2,1)S(1)}, u32[]{:S(2)}) copy-start(bf16[512,768]{1,0:T(8,128)(2,1)S(1)} %convolution_convert_fusion.2.refs_1_) | copy-start | bytes 2359300
  35.0 2.5 %copy-start.6 = (s32[1024]{0:T(1024)S(1)}, s32[1024]{0:T(1024)}, u32[]{:S(2)}) copy-start(s32[1024]{0:T(1024)} %param.7) | copy-start | bytes 12292
  54.3 1.4 copy-start.2
  55.7 1.9 %copy-start.1 = (bf16[1024,512]{1,0:T(8,128)(2,1)}, bf16[1024,512]{1,0:T(8,128)(2,1)S(1)}, u32[]{:S(2)}) copy-start(bf16[1024,512]{1,0:T(8,128)(2,1)S(1)} %fusion.3.refs_0_) | copy-start | bytes 3145732
  55.7 85.5 %slice-start = ((s8[6291456]{0:T(1024)(128)(4,1)}), s8[4194304]{0:T(1024)(128)(4,1)S(1)}, s32[]{:S(2)}) async-start(s8[6291456]{0:T(1024)(128)(4,1)} %bitcast.28), calls=%async_computation | async-start | bytes 8388608
  57.6 83.5 %slice-start.1 = ((s8[6291456]{0:T(1024)(128)(4,1)}), s8[2097152]{0:T(1024)(128)(4,1)S(1)}, s32[]{:S(2)}) async-start(s8[6291456]{0:T(1024)(128)(4,1)} %bitcast.28), calls=%async_computation.1 | async-start | bytes 4194304
  83.1 58.1 %copy-start.5 = (bf16[32,768]{1,0:T(8,128)(2,1)S(1)}, bf16[32,768]{1,0:T(8,128)(2,1)}, u32[]{:S(2)}) copy-start(bf16[32,768]{1,0:T(8,128)(2,1)} %convert_element_type.26.refs_3_) | copy-start | bytes 147460
  141.2 2.7 %copy-start.3 = (f32[128,768]{1,0:T(8,128)S(1)}, f32[128,768]{1,0:T(8,128)}, u32[]{:S(2)}) copy-start(f32[128,768]{1,0:T(8,128)} %shard_map.70) | copy-start | bytes 1179652

commit v2 on v1

--- a/solution.py
+++ b/solution.py
@@ -75,7 +75,9 @@
     return table, count
 
 
-def gather_kernel(grid, orders, table, x_ref, o_ref, send_sem, recv_sem):
+def gather_kernel(grid, orders, table, beside, n_extra, x_ref, *refs):
+    extra, o_ref, beside_ref = refs[:n_extra], refs[n_extra], refs[n_extra + 1]
+    send_sem, recv_sem = refs[n_extra + 2 :]
     row, col, mine = grid.place()
     greet(grid, row, col, mine)
     o_ref[tuple(mine)] = x_ref[...]
@@ -123,6 +125,7 @@
 
     for part in range(len(orders)):
         start(part, 0)
+    beside(*extra, beside_ref)
     steps = len(grid.sizes)
     for step in range(steps):
         for part in range(len(orders)):
@@ -133,58 +136,94 @@
         copy.wait_send()
 
 
-def gather(grid, x, cuts, collective_id):
+def gather(grid, x, cuts, beside, extra, beside_shape, collective_id):
     rows, cols = x.shape
     orders = []
     for part, (first, last) in enumerate(zip(cuts[:-1], cuts[1:])):
         orders.append((first, last, [0] + grid.middle(part) + [grid.core]))
     table, count = semaphore_table(grid, orders)
-    out = pl.pallas_call(
-        functools.partial(gather_kernel, grid, orders, table),
-        out_shape=jax.ShapeDtypeStruct(tuple(grid.sizes) + (rows, cols), x.dtype),
-        in_specs=[pl.BlockSpec(memory_space=pltpu.VMEM)],
-        out_specs=pl.BlockSpec(memory_space=pltpu.VMEM),
+    out, made = pl.pallas_call(
+        functools.partial(gather_kernel, grid, orders, table, beside, len(extra)),
+        out_shape=(
+            jax.ShapeDtypeStruct(tuple(grid.sizes) + (rows, cols), x.dtype),
+            jax.ShapeDtypeStruct(beside_shape, jnp.bfloat16),
+        ),
+        in_specs=[pl.BlockSpec(memory_space=pltpu.VMEM)] * (1 + len(extra)),
+        out_specs=[pl.BlockSpec(memory_space=pltpu.VMEM)] * 2,
         scratch_shapes=[pltpu.SemaphoreType.DMA((count,)), pltpu.SemaphoreType.DMA((count,))],
         compiler_params=pltpu.CompilerParams(
             collective_id=collective_id, has_side_effects=True, vmem_limit_bytes=LIMIT
         ),
-    )(x)
-    return out.reshape(grid.n_row * grid.n_col, rows, cols)
-
-
-def reduce_kernel(grid, orders, table, produce, n_in, *refs):
-    ins, out_ref = refs[:n_in], refs[n_in]
-    total, core_out, core_in = refs[n_in + 1 : n_in + 4]
-    core_send, core_recv, send_sem, recv_sem = refs[n_in + 4 : n_in + 8]
-    n_parts = len(orders)
-    outgoing = refs[n_in + 8 : n_in + 8 + len(table)]
-    incoming = refs[n_in + 8 + len(table) :]
+    )(x, *extra)
+    return out.reshape(grid.n_row * grid.n_col * rows, cols), made
+
+
+def stats_kernel(grid, dims, x_ref, o_ref, state, incoming, send_sem, recv_sem):
     row, col, mine = grid.place()
     greet(grid, row, col, mine)
-    core = grid.core
+    started, slot = [], 0
+    top, total, picked = x_ref[0], x_ref[1], x_ref[2]
+    for step, dim in enumerate(dims):
+        state[step, 0], state[step, 1], state[step, 2] = top, total, picked
+        copies = []
+        for offset in range(1, grid.sizes[dim]):
+            copy = pltpu.make_async_remote_copy(
+                src_ref=state.at[step],
+                dst_ref=incoming.at[slot],
+                send_sem=send_sem.at[slot],
+                recv_sem=recv_sem.at[slot],
+                device_id=grid.partner(row, col, mine, dim, grid.moved(mine, dim, offset)),
+                device_id_type=MESH,
+            )
+            copy.start()
+            copies.append((slot, copy))
+            slot += 1
+        for at, copy in copies:
+            copy.wait_recv()
+            theirs = incoming[at, 0]
+            higher = jnp.maximum(top, theirs)
+            total = total * jnp.exp(top - higher) + incoming[at, 1] * jnp.exp(theirs - higher)
+            picked = picked + incoming[at, 2]
+            top = higher
+            started.append(copy)
+    o_ref[0] = top + jnp.log(total)
+    o_ref[1] = picked
+    for copy in started:
+        copy.wait_send()
+
+
+def combine_stats(grid, stats, collective_id):
+    dims = list(range(grid.core, -1, -1))
+    slots = sum(size - 1 for size in grid.sizes)
+    return pl.pallas_call(
+        functools.partial(stats_kernel, grid, dims),
+        out_shape=jax.ShapeDtypeStruct((2,) + stats.shape[1:], jnp.float32),
+        in_specs=[pl.BlockSpec(memory_space=pltpu.VMEM)],
+        out_specs=pl.BlockSpec(memory_space=pltpu.VMEM),
+        scratch_shapes=[
+            pltpu.VMEM((len(dims),) + stats.shape, jnp.float32),
+            pltpu.VMEM((slots,) + stats.shape, jnp.float32),
+            pltpu.SemaphoreType.DMA((slots,)),
+            pltpu.SemaphoreType.DMA((slots,)),
+        ],
+        compiler_params=pltpu.CompilerParams(collective_id=collective_id, has_side_effects=True),
+    )(stats)
+
+
+def reduce_kernel(grid, orders, table, produce, beside, n_in, n_extra, *refs):
+    ins, extra = refs[:n_in], refs[n_in : n_in + n_extra]
+    refs = refs[n_in + n_extra :]
+    out_ref, beside_ref, total, core_out, core_in = refs[:5]
+    core_send, core_recv, send_sem, recv_sem = refs[5:9]
+    outgoing, incoming = refs[9 : 9 + len(table)], refs[9 + len(table) :]
+    row, col, mine = grid.place()
+    greet(grid, row, col, mine)
+    core, n_row = grid.core, grid.n_row
     other = 1 - mine[core]
     between = (slice(None),) * (core - 1)
     shape = total.shape[1:]
-    core_copies = []
-    for z in range(grid.n_row):
-        total[z] = produce(z, *ins).reshape(shape)
-        core_out[z] = total[(z,) + between + (other,)].astype(jnp.bfloat16)
-        copy = pltpu.make_async_remote_copy(
-            src_ref=core_out.at[z],
-            dst_ref=core_in.at[z],
-            send_sem=core_send.at[z],
-            recv_sem=core_recv.at[z],
-            device_id=grid.partner(row, col, mine, core, other),
-            device_id_type=MESH,
-        )
-        copy.start()
-        core_copies.append(copy)
-    for z, copy in enumerate(core_copies):
-        copy.wait_recv()
-        where = (z,) + between + (mine[core],)
-        total[where] = total[where] + core_in[z].astype(jnp.float32)
-
-    started = []
+    slabs = [grid.moved(mine, 0, turn + 1) for turn in range(n_row)]
+    started, waiting = [], {}
 
     def region(part, step, value):
         first, last, order = orders[part]
@@ -194,52 +233,94 @@
             index.append(value if d == dim else mine[d] if d in done else slice(None))
         return tuple(index) + (mine[core], pl.ds(first, last - first))
 
-    def start(part, step):
+    def send(part, step, offset, turn=None):
         dim = orders[part][2][step]
-        for offset in range(1, grid.sizes[dim]):
-            sem = table[part, dim, offset]
-            value = grid.moved(mine, dim, offset)
-            outgoing[sem][...] = total[region(part, step, value)].astype(jnp.bfloat16)
-            copy = pltpu.make_async_remote_copy(
-                src_ref=outgoing[sem],
-                dst_ref=incoming[sem],
-                send_sem=send_sem.at[sem],
-                recv_sem=recv_sem.at[sem],
-                device_id=grid.partner(row, col, mine, dim, value),
-                device_id_type=MESH,
-            )
-            copy.start()
-            started.append(copy)
-            waiting[part, step, offset] = copy
+        entry = table[part, dim, offset]
+        value = grid.moved(mine, dim, offset)
+        where = region(part, step, value)
+        source, target, sem = outgoing[entry], incoming[entry], entry * n_row
+        if turn is not None:
+            where = (slabs[turn],) + where[1:]
+            source, target, sem = source.at[turn], target.at[turn], sem + turn
+        source[...] = total[where].astype(jnp.bfloat16)
+        copy = pltpu.make_async_remote_copy(
+            src_ref=source,
+            dst_ref=target,
+            send_sem=send_sem.at[sem],
+            recv_sem=recv_sem.at[sem],
+            device_id=grid.partner(row, col, mine, dim, value),
+            device_id_type=MESH,
+        )
+        copy.start()
+        started.append(copy)
+        waiting[part, step, offset, turn] = copy
+
+    def core_start(turn):
+        z = slabs[turn]
+        total[z] = produce(z, *ins).reshape(shape)
+        core_out[turn] = total[(z,) + between + (other,)].astype(jnp.bfloat16)
+        copy = pltpu.make_async_remote_copy(
+            src_ref=core_out.at[turn],
+            dst_ref=core_in.at[turn],
+            send_sem=core_send.at[turn],
+            recv_sem=core_recv.at[turn],
+            device_id=grid.partner(row, col, mine, core, other),
+            device_id_type=MESH,
+        )
+        copy.start()
+        started.append(copy)
+        waiting[turn] = copy
+
+    def core_finish(turn):
+        waiting[turn].wait_recv()
+        where = (slabs[turn],) + between + (mine[core],)
+        total[where] = total[where] + core_in[turn].astype(jnp.float32)
+        for part, (_, _, order) in enumerate(orders):
+            if order[0] != 0:
+                for offset in range(1, grid.sizes[order[0]]):
+                    send(part, 0, offset, turn)
+            elif turn + 1 < n_row:
+                send(part, 0, turn + 1)
 
     def finish(part, step):
         dim = orders[part][2][step]
-        where = region(part, step, mine[dim])
-        value = total[where]
-        for offset in range(1, grid.sizes[dim]):
-            waiting[part, step, offset].wait_recv()
-            value = value + incoming[table[part, dim, offset]][...].astype(jnp.float32)
-        total[where] = value
-
-    waiting = {}
-    for part in range(n_parts):
-        start(part, 0)
+        split = step == 0 and dim != 0
+        for turn in range(n_row) if split else (None,):
+            where = region(part, step, mine[dim])
+            if split:
+                where = (slabs[turn],) + where[1:]
+            value = total[where]
+            for offset in range(1, grid.sizes[dim]):
+                waiting[part, step, offset, turn].wait_recv()
+                landed = incoming[table[part, dim, offset]]
+                landed = landed[turn] if split else landed[...]
+                value = value + landed.astype(jnp.float32)
+            total[where] = value
+
+    for turn in range(n_row):
+        core_start(turn)
+        if turn:
+            core_finish(turn - 1)
+    core_finish(n_row - 1)
+    beside(*extra, beside_ref)
     steps = core
     turns = []
-    for part in range(n_parts):
+    for part in range(len(orders)):
         late = 1.5 if orders[part][2][0] == 0 else 0
         for step in range(steps):
             turns.append((step + late, part, step))
     for _, part, step in sorted(turns):
         finish(part, step)
         if step + 1 < steps:
-            start(part, step + 1)
+            dim = orders[part][2][step + 1]
+            for offset in range(1, grid.sizes[dim]):
+                send(part, step + 1, offset)
     out_ref[...] = total[tuple(mine)]
-    for copy in core_copies + started:
+    for copy in started:
         copy.wait_send()
 
 
-def reduce_scatter(grid, produce, ins, rows, cols, plan, collective_id):
+def reduce_scatter(grid, produce, ins, beside, extra, beside_shape, rows, cols, plan, collective_id):
     core = grid.core
     orders = []
     for first, last, turn, row_first in plan:
@@ -255,25 +336,30 @@
     sizes = tuple(grid.sizes)
     half = pltpu.VMEM(sizes[:-1] + (rows, cols), jnp.bfloat16)
     return pl.pallas_call(
-        functools.partial(reduce_kernel, grid, orders, table, produce, len(ins)),
-        out_shape=jax.ShapeDtypeStruct((rows, cols), jnp.float32),
-        in_specs=[pl.BlockSpec(memory_space=pltpu.VMEM)] * len(ins),
-        out_specs=pl.BlockSpec(memory_space=pltpu.VMEM),
+        functools.partial(
+            reduce_kernel, grid, orders, table, produce, beside, len(ins), len(extra)
+        ),
+        out_shape=(
+            jax.ShapeDtypeStruct((rows, cols), jnp.float32),
+            jax.ShapeDtypeStruct(beside_shape, jnp.bfloat16),
+        ),
+        in_specs=[pl.BlockSpec(memory_space=pltpu.VMEM)] * (len(ins) + len(extra)),
+        out_specs=[pl.BlockSpec(memory_space=pltpu.VMEM)] * 2,
         scratch_shapes=[
             pltpu.VMEM(sizes + (rows, cols), jnp.float32),
             half,
             half,
             pltpu.SemaphoreType.DMA((grid.n_row,)),
             pltpu.SemaphoreType.DMA((grid.n_row,)),
-            pltpu.SemaphoreType.DMA((count,)),
-            pltpu.SemaphoreType.DMA((count,)),
+            pltpu.SemaphoreType.DMA((count * grid.n_row,)),
+            pltpu.SemaphoreType.DMA((count * grid.n_row,)),
         ]
         + buffers
         + buffers,
         compiler_params=pltpu.CompilerParams(
             collective_id=collective_id, has_side_effects=True, vmem_limit_bytes=LIMIT
         ),
-    )(*ins)
+    )(*ins, *extra)
 
 
 def contract_first(left, right):
@@ -284,17 +370,51 @@
 
 def query_slab(z, height, dscores_ref, pa_ref):
     return jnp.dot(
-        dscores_ref[z * height : (z + 1) * height, :],
+        dscores_ref[pl.ds(pl.multiple_of(z * height, height), height), :],
         pa_ref[...],
         preferred_element_type=jnp.float32,
     )
 
 
 def adapter_slab(z, width, passages_ref, dpa_ref, queries_ref, dqa_ref):
-    columns = slice(z * width, (z + 1) * width)
+    columns = pl.ds(pl.multiple_of(z * width, width), width)
     return contract_first(passages_ref[:, columns], dpa_ref[...]) + contract_first(
         queries_ref[:, columns], dqa_ref[...]
     )
+
+
+def adapt(passages_ref, adapter_ref, pa_ref):
+    block = min(256, pa_ref.shape[0])
+
+    @pl.loop(0, pa_ref.shape[0] // block)
+    def _(step):
+        rows = pl.ds(pl.multiple_of(step * block, block), block)
+        pa_ref[rows, :] = jnp.dot(
+            passages_ref[rows, :], adapter_ref[...], preferred_element_type=jnp.float32
+        ).astype(jnp.bfloat16)
+
+
+def passage_grad(dscores_ref, qa_ref, dpa_ref):
+    block = min(256, dpa_ref.shape[0])
+
+    @pl.loop(0, dpa_ref.shape[0] // block)
+    def _(step):
+        rows = pl.ds(pl.multiple_of(step * block, block), block)
+        dpa_ref[rows, :] = contract_first(dscores_ref[:, rows], qa_ref[...]).astype(jnp.bfloat16)
+
+
+def query_back(dqa_ref, adapter_ref, grad_ref):
+    block = min(512, grad_ref.shape[1])
+
+    @pl.loop(0, grad_ref.shape[1] // block)
+    def _(step):
+        columns = pl.ds(pl.multiple_of(step * block, block), block)
+        grad_ref[:, columns] = lax.dot_general(
+            dqa_ref[...],
+            adapter_ref[columns, :],
+            (((1,), (1,)), ((), ())),
+            preferred_element_type=jnp.float32,
+        ).astype(jnp.bfloat16)
 
 
 def thirds(rows):
@@ -321,9 +441,8 @@
     n_query = own_rows * n
     here = lax.axis_index(("row", "col"))
     local_qa = jnp.dot(queries, adapter, preferred_element_type=jnp.float32).astype(jnp.bfloat16)
-    pa = jnp.dot(passages, adapter, preferred_element_type=jnp.float32).astype(jnp.bfloat16)
     cuts = [0, own_rows // 2, own_rows] if own_rows % 32 == 0 else [0, own_rows]
-    qa = gather(grid, local_qa, cuts, 0).reshape(n_query, emb)
+    qa, pa = gather(grid, local_qa, cuts, adapt, (passages, adapter), (slab_rows, emb), 0)
     scores = (
         lax.dot_general(qa, pa, (((1,), (1,)), ((), ())), preferred_element_type=jnp.float32)
         * scale
@@ -333,31 +452,30 @@
     local_max = jnp.max(scores, axis=1)
     local_pos = jnp.sum(jnp.where(hit, scores, 0.0), axis=1)
     local_sum = jnp.sum(jnp.exp(scores - local_max[:, None]), axis=1)
-    stats = jnp.stack([local_max, local_sum, local_pos]).reshape(-1, 128)
-    stats = gather(grid, stats, [0, 8, stats.shape[0]], 1).reshape(n, 3, n_query)
-    top = jnp.max(stats[:, 0], axis=0)
-    total = jnp.sum(stats[:, 1] * jnp.exp(stats[:, 0] - top), axis=0)
-    picked = jnp.sum(stats[:, 2], axis=0)
-    lse = top + jnp.log(total)
+    stats = jnp.stack([local_max, local_sum, local_pos]).reshape(3, -1, 128)
+    lse, picked = combine_stats(grid, stats, 1).reshape(2, n_query)
     probs = jnp.exp(scores - lse[:, None])
     dscores = ((probs - hit.astype(jnp.float32)) * scale).astype(jnp.bfloat16)
-    dqa_own = reduce_scatter(
+    dqa_own, dpa = reduce_scatter(
         grid,
         lambda z, *refs: query_slab(z, n_query // grid.n_row, *refs),
         (dscores, pa),
+        lambda qa_ref, dscores_ref, dpa_ref: passage_grad(dscores_ref, qa_ref, dpa_ref),
+        (qa, dscores),
+        (slab_rows, emb),
         own_rows,
         emb,
         thirds(own_rows),
         2,
-    ).astype(jnp.bfloat16)
-    dpa = contract_first(dscores, qa).astype(jnp.bfloat16)
-    query_grad = lax.dot_general(
-        dqa_own, adapter, (((1,), (1,)), ((), ())), preferred_element_type=jnp.float32
-    ).astype(jnp.bfloat16)
-    adapter_grad = reduce_scatter(
+    )
+    dqa_own = dqa_own.astype(jnp.bfloat16)
+    adapter_grad, query_grad = reduce_scatter(
         grid,
         lambda z, *refs: adapter_slab(z, width // grid.n_row, *refs),
         (passages, dpa, queries, dqa_own),
+        query_back,
+        (dqa_own, adapter),
+        (own_rows, width),
         width // n,
         emb,
         thirds(width // n),

time: 145 us -> 133 us (0.917)
  matrix products: 17.5 us -> 7.33 us
  Pallas kernels: 119 us -> 115 us
  other arithmetic: 3.45 us -> 5.3 us
    dot_general x3 -> x0, matrix products: 10.2 us -> none  [the longest x1 5.63 us: per_device(): jnp.dot(passages, adapter, preferred_element_type=jnp.float32)]
    pallas_call x2, Pallas kernels: 81.4 us -> 74.8 us  [reduce_scatter(): pl.pallas_call(functools.partial(reduce_kernel, grid, orders, table, prod...]
    unnamed x19 -> x4, local copies, waits for them, and re-layouts: 1.12 us -> 3.44 us
    pallas_call x2, Pallas kernels: 38 us -> 39.8 us  [the longest x1 27.3 us: gather(): pl.pallas_call(functools.partial(gather_kernel, grid, orders, table, besi...]
where the time goes in v2:
time: 133 us
  Pallas kernels  115 us (86%)
  matrix products  7.33 us (6%)
  other arithmetic  5.3 us (4%)
  local copies, waits for them, and re-layouts  4.71 us (4%)
    pallas_call x2, Pallas kernels, reduce_scatter(): pl.pallas_call(functools.partial(reduce_kernel, grid, orders, table, prod...  74.8 us
    pallas_call x1, Pallas kernels, gather(): pl.pallas_call(functools.partial(gather_kernel, grid, orders, table, besi...  27.3 us
    pallas_call x1, Pallas kernels, combine_stats(): pl.pallas_call(functools.partial(stats_kernel, grid, dims), out_shape=jax...  12.5 us
    dot_general x1, matrix products, per_device(): jnp.dot(queries, adapter, preferred_element_type=jnp.float32)  4.64 us
    unnamed x4, local copies, waits for them, and re-layouts  3.44 us
    dot_general x1, matrix products, per_device(): lax.dot_general(qa, pa, (((1,), (1,)), ((), ())), preferred_element_type=...  2.7 us

profile of v2, /device:TPU:0, one launch (start us, length us, event | category | flops | bytes accessed | tf_op | source)
XLA Modules:
  0.0 132.6 jit_solution(16903363433655657613)
XLA Ops:
  0.6 4.6 %convolution_convert_fusion.x_ref = bf16[32,768]{1,0:T(8,128)(2,1)} fusion(bf16[32,4096]{1,0:T(8,128)(2,1)} %refs_2_.1, bf16[4096,768]{1,0:T(8,128)(2,1)} %refs_5_.1), kind=kOutput, calls=%fused_computation.8 | convolution fusion | flops 201351168 | bytes 6602752 | tf_op jit(solution)/shard_map/dot_general | solution.py:443
  5.3 27.3 %shard_map.67 = (bf16[4,2,2,2,32,768]{5,4,3,2,1,0:T(8,128)(2,1)}, bf16[512,768]{1,0:T(8,128)(2,1)}) custom-call(bf16[32,768]{1,0:T(8,128)(2,1)} %convolution_convert_fusion.x_ref, bf16[512,4096]{1,0:T(8,128)(2,1)} %refs_0_.3, bf16[4096,768]{1,0:T(8,128)(2,1)} %refs_5_.1), custom_call_target="tpu_custom_call" | custom-call | tf_op jit(solution)/shard_map/pallas_call | solution.py:145
  32.6 0.0 copy-start
  32.6 2.7 %multiply_reduce_fusion = (f32[1024]{0:T(1024)S(1)}, f32[1024,512]{1,0:T(8,128)S(1)}) fusion(bf16[1024,768]{1,0:T(8,128)(2,1)} %bitcast.14, bf16[512,768]{1,0:T(8,128)(2,1)} %get-tuple-element.10.refs_1_), kind=kOutput, calls=%fused_computation.7 | convolution fusion | flops 806353920 | bytes 4460544 | tf_op jit(solution)/shard_map/dot_general | solution.py:447
  35.3 0.0 copy-done
  35.3 0.9 exponential_reduce_fusion
  36.2 0.6 pad_maximum_fusion.x_ref
  36.8 12.5 %shard_map.68 = f32[2,8,128]{2,1,0:T(8,128)} custom-call(f32[3,8,128]{2,1,0:T(8,128)} %pad_maximum_fusion.x_ref), custom_call_target="tpu_custom_call" | custom-call | tf_op jit(solution)/shard_map/pallas_call | solution.py:198
  49.3 0.7 bitcast_subtract_fusion
  50.0 0.7 slice_bitcast_fusion
  50.7 1.6 %fusion.3.refs_0_.refs_3_ = bf16[1024,512]{1,0:T(8,128)(2,1)} fusion(f32[1024,512]{1,0:T(8,128)S(1)} %get-tuple-element.18, f32[1024]{0:T(1024)S(1)} %slice_bitcast_fusion, s32[512]{0:T(512)S(1)} %iota_add_fusion, s32[1024]{0:T(1024)S(1)} %copy-done), kind=kLoop, calls=%fused_computation.5 | loop fusion | flops 3670016 | bytes 3155968 | tf_op jit(solution)/shard_map/convert_element_type | solution.py:458
  52.3 23.5 %shard_map.69 = (f32[32,768]{1,0:T(8,128)}, bf16[512,768]{1,0:T(8,128)(2,1)}) custom-call(bf16[1024,512]{1,0:T(8,128)(2,1)} %fusion.3.refs_0_.refs_3_, bf16[512,768]{1,0:T(8,128)(2,1)} %get-tuple-element.10.refs_1_, bf16[1024,768]{1,0:T(8,128)(2,1)} %bitcast.15, bf16[1024,512]{1,0:T(8,128)(2,1)} %fusion.3.refs_0_.refs_3_), custom_call_target="tpu_custom_call" | custom-call | tf_op jit(solution)/shard_map/pallas_call | solution.py:338
  75.8 0.6 dynamic_slice.3
  76.4 1.5 %convert_element_type.15.refs_3_.refs_4_ = bf16[32,768]{1,0:T(8,128)(2,1)} convert(f32[32,768]{1,0:T(8,128)} %get-tuple-element.12) | non-fusion elementwise | flops 24576 | bytes 147456 | tf_op jit(solution)/shard_map/convert_element_type | solution.py:471
  77.9 51.2 %shard_map.70 = (f32[128,768]{1,0:T(8,128)}, bf16[32,4096]{1,0:T(8,128)(2,1)}) custom-call(bf16[512,4096]{1,0:T(8,128)(2,1)} %refs_0_.3, bf16[512,768]{1,0:T(8,128)(2,1)} %get-tuple-element.11.refs_1_, bf16[32,4096]{1,0:T(8,128)(2,1)} %refs_2_.1, bf16[32,768]{1,0:T(8,128)(2,1)} %convert_element_type.15.refs_3_.refs_4_, ...), custom_call_target="tpu_custom_call" | custom-call | tf_op jit(solution)/shard_map/pallas_call | solution.py:338
  129.2 1.8 %copy.11 = f32[128,768]{1,0:T(8,128)} copy(f32[128,768]{1,0:T(8,128)} %get-tuple-element.22) | data formatting | bytes 786432
  131.0 1.7 %copy.12 = bf16[32,4096]{1,0:T(8,128)(2,1)} copy(bf16[32,4096]{1,0:T(8,128)(2,1)} %get-tuple-element.23) | data formatting | bytes 524288
  (1 shorter events, 0.0 us)
Async XLA Ops:
  32.6 2.7 %copy-start = (s32[1024]{0:T(1024)S(1)}, s32[1024]{0:T(1024)}, u32[]{:S(2)}) copy-start(s32[1024]{0:T(1024)} %param.7) | copy-start | bytes 12292

commit v3 on v2

--- a/solution.py
+++ b/solution.py
@@ -125,13 +125,15 @@
 
     for part in range(len(orders)):
         start(part, 0)
-    beside(*extra, beside_ref)
+    beside(0, *extra, beside_ref)
     steps = len(grid.sizes)
     for step in range(steps):
         for part in range(len(orders)):
             finish(part, step)
             if step + 1 < steps:
                 start(part, step + 1)
+        if step + 1 < steps:
+            beside(step + 1, *extra, beside_ref)
     for copy in started:
         copy.wait_send()
 
@@ -225,35 +227,45 @@
     slabs = [grid.moved(mine, 0, turn + 1) for turn in range(n_row)]
     started, waiting = [], {}
 
-    def region(part, step, value):
+    def region(part, step, turn, value):
         first, last, order = orders[part]
         dim, done = order[step], order[:step]
-        index = []
-        for d in range(core):
+        index = [slabs[turn]]
+        for d in range(1, core):
             index.append(value if d == dim else mine[d] if d in done else slice(None))
         return tuple(index) + (mine[core], pl.ds(first, last - first))
 
-    def send(part, step, offset, turn=None):
+    def send(part, step, turn):
         dim = orders[part][2][step]
-        entry = table[part, dim, offset]
-        value = grid.moved(mine, dim, offset)
-        where = region(part, step, value)
-        source, target, sem = outgoing[entry], incoming[entry], entry * n_row
-        if turn is not None:
-            where = (slabs[turn],) + where[1:]
-            source, target, sem = source.at[turn], target.at[turn], sem + turn
-        source[...] = total[where].astype(jnp.bfloat16)
-        copy = pltpu.make_async_remote_copy(
-            src_ref=source,
-            dst_ref=target,
-            send_sem=send_sem.at[sem],
-            recv_sem=recv_sem.at[sem],
-            device_id=grid.partner(row, col, mine, dim, value),
-            device_id_type=MESH,
-        )
-        copy.start()
-        started.append(copy)
-        waiting[part, step, offset, turn] = copy
+        offsets = (turn + 1,) if dim == 0 else range(1, grid.sizes[dim])
+        for offset in offsets:
+            entry = table[part, dim, offset]
+            value = grid.moved(mine, dim, offset)
+            source, target, sem = outgoing[entry], incoming[entry], entry * n_row
+            if dim != 0:
+                source, target, sem = source.at[turn], target.at[turn], sem + turn
+            source[...] = total[region(part, step, turn, value)].astype(jnp.bfloat16)
+            copy = pltpu.make_async_remote_copy(
+                src_ref=source,
+                dst_ref=target,
+                send_sem=send_sem.at[sem],
+                recv_sem=recv_sem.at[sem],
+                device_id=grid.partner(row, col, mine, dim, value),
+                device_id_type=MESH,
+            )
+            copy.start()
+            started.append(copy)
+            waiting[part, step, turn, offset] = copy
+
+    def finish(part, step, turn):
+        dim = orders[part][2][step]
+        where = region(part, step, turn, mine[dim])
+        value = total[where]
+        for offset in range(1, grid.sizes[dim]):
+            waiting[part, step, turn, offset].wait_recv()
+            landed = incoming[table[part, dim, offset]][turn]
+            value = value + landed.astype(jnp.float32)
+        total[where] = value
 
     def core_start(turn):
         z = slabs[turn]
@@ -275,27 +287,12 @@
         waiting[turn].wait_recv()
         where = (slabs[turn],) + between + (mine[core],)
         total[where] = total[where] + core_in[turn].astype(jnp.float32)
-        for part, (_, _, order) in enumerate(orders):
-            if order[0] != 0:
-                for offset in range(1, grid.sizes[order[0]]):
-                    send(part, 0, offset, turn)
-            elif turn + 1 < n_row:
-                send(part, 0, turn + 1)
-
-    def finish(part, step):
-        dim = orders[part][2][step]
-        split = step == 0 and dim != 0
-        for turn in range(n_row) if split else (None,):
-            where = region(part, step, mine[dim])
-            if split:
-                where = (slabs[turn],) + where[1:]
-            value = total[where]
-            for offset in range(1, grid.sizes[dim]):
-                waiting[part, step, offset, turn].wait_recv()
-                landed = incoming[table[part, dim, offset]]
-                landed = landed[turn] if split else landed[...]
-                value = value + landed.astype(jnp.float32)
-            total[where] = value
+        for part in range(len(orders)):
+            follow(part, 0, turn)
+
+    def follow(part, step, turn):
+        if step < core - 1 or turn + 1 < n_row:
+            send(part, step, turn)
 
     for turn in range(n_row):
         core_start(turn)
@@ -303,29 +300,27 @@
             core_finish(turn - 1)
     core_finish(n_row - 1)
     beside(*extra, beside_ref)
-    steps = core
-    turns = []
-    for part in range(len(orders)):
-        late = 1.5 if orders[part][2][0] == 0 else 0
-        for step in range(steps):
-            turns.append((step + late, part, step))
-    for _, part, step in sorted(turns):
-        finish(part, step)
-        if step + 1 < steps:
-            dim = orders[part][2][step + 1]
-            for offset in range(1, grid.sizes[dim]):
-                send(part, step + 1, offset)
-    out_ref[...] = total[tuple(mine)]
+    turns = [(turn + step, turn, step) for turn in range(n_row) for step in range(core - 1)]
+    for _, turn, step in sorted(turns):
+        for part in range(len(orders)):
+            finish(part, step, turn)
+            follow(part, step + 1, turn)
+    for part, (first, last, _) in enumerate(orders):
+        where = tuple(mine) + (pl.ds(first, last - first),)
+        value = total[where]
+        for offset in range(1, n_row):
+            waiting[part, core - 1, offset - 1, offset].wait_recv()
+            value = value + incoming[table[part, 0, offset]][...].astype(jnp.float32)
+        out_ref[first:last, :] = value
     for copy in started:
         copy.wait_send()
 
 
-def reduce_scatter(grid, produce, ins, beside, extra, beside_shape, rows, cols, plan, collective_id):
+def reduce_scatter(grid, produce, ins, beside, extra, beside_shape, rows, cols, cuts, collective_id):
     core = grid.core
     orders = []
-    for first, last, turn, row_first in plan:
-        middle = grid.middle(turn)
-        orders.append((first, last, [0] + middle if row_first else middle + [0]))
+    for turn, (first, last) in enumerate(zip(cuts[:-1], cuts[1:])):
+        orders.append((first, last, grid.middle(turn) + [0]))
     table, count = semaphore_table(grid, orders)
     buffers = []
     for part, (first, last, order) in enumerate(orders):
@@ -383,12 +378,10 @@
     )
 
 
-def adapt(passages_ref, adapter_ref, pa_ref):
-    block = min(256, pa_ref.shape[0])
-
-    @pl.loop(0, pa_ref.shape[0] // block)
-    def _(step):
-        rows = pl.ds(pl.multiple_of(step * block, block), block)
+def adapt(step, passages_ref, adapter_ref, pa_ref):
+    block = pa_ref.shape[0] // 2
+    if step < 2:
+        rows = slice(step * block, (step + 1) * block)
         pa_ref[rows, :] = jnp.dot(
             passages_ref[rows, :], adapter_ref[...], preferred_element_type=jnp.float32
         ).astype(jnp.bfloat16)
@@ -417,19 +410,8 @@
         ).astype(jnp.bfloat16)
 
 
-def thirds(rows):
-    unit = rows // 16
-    large = (unit * 3) // 8
-    if large == 0:
-        half = (unit // 2) * 16
-        if half == 0:
-            return [(0, rows, 0, False)]
-        return [(0, half, 0, False), (half, rows, 1, False)]
-    return [
-        (0, 16 * large, 0, False),
-        (16 * large, 32 * large, 1, False),
-        (32 * large, rows, 0, True),
-    ]
+def halves(rows):
+    return [0, rows // 2, rows] if rows % 32 == 0 else [0, rows]
 
 
 def per_device(grid, queries, passages, adapter, positives):
@@ -441,8 +423,7 @@
     n_query = own_rows * n
     here = lax.axis_index(("row", "col"))
     local_qa = jnp.dot(queries, adapter, preferred_element_type=jnp.float32).astype(jnp.bfloat16)
-    cuts = [0, own_rows // 2, own_rows] if own_rows % 32 == 0 else [0, own_rows]
-    qa, pa = gather(grid, local_qa, cuts, adapt, (passages, adapter), (slab_rows, emb), 0)
+    qa, pa = gather(grid, local_qa, halves(own_rows), adapt, (passages, adapter), (slab_rows, emb), 0)
     scores = (
         lax.dot_general(qa, pa, (((1,), (1,)), ((), ())), preferred_element_type=jnp.float32)
         * scale
@@ -465,7 +446,7 @@
         (slab_rows, emb),
         own_rows,
         emb,
-        thirds(own_rows),
+        halves(own_rows),
         2,
     )
     dqa_own = dqa_own.astype(jnp.bfloat16)
@@ -478,7 +459,7 @@
         (own_rows, width),
         width // n,
         emb,
-        thirds(width // n),
+        halves(width // n),
         3,
     )
     first_row = here * own_rows

time: 133 us -> 134 us (level)
    pallas_call x2, Pallas kernels: 74.8 us -> 76.1 us  [reduce_scatter(): pl.pallas_call(functools.partial(reduce_kernel, grid, orders, table, prod...]
where the time goes in v3:
time: 134 us
  Pallas kernels  116 us (87%)
  matrix products  7.33 us (5%)
  other arithmetic  5.3 us (4%)
  local copies, waits for them, and re-layouts  4.71 us (4%)
    pallas_call x2, Pallas kernels, reduce_scatter(): pl.pallas_call(functools.partial(reduce_kernel, grid, orders, table, prod...  76.1 us
    pallas_call x1, Pallas kernels, gather(): pl.pallas_call(functools.partial(gather_kernel, grid, orders, table, besi...  27 us
    pallas_call x1, Pallas kernels, combine_stats(): pl.pallas_call(functools.partial(stats_kernel, grid, dims), out_shape=jax...  12.7 us
    dot_general x1, matrix products, per_device(): jnp.dot(queries, adapter, preferred_element_type=jnp.float32)  4.64 us
    unnamed x4, local copies, waits for them, and re-layouts  3.44 us
    dot_general x1, matrix products, per_device(): lax.dot_general(qa, pa, (((1,), (1,)), ((), ())), preferred_element_type=...  2.7 us

profile of v3, /device:TPU:0, one launch (start us, length us, event | category | flops | bytes accessed | tf_op | source)
XLA Modules:
  0.0 133.9 jit_solution(9240600252967736982)
XLA Ops:
  0.6 4.6 %convolution_convert_fusion.x_ref = bf16[32,768]{1,0:T(8,128)(2,1)} fusion(bf16[32,4096]{1,0:T(8,128)(2,1)} %refs_2_.1, bf16[4096,768]{1,0:T(8,128)(2,1)} %refs_5_.1), kind=kOutput, calls=%fused_computation.8 | convolution fusion | flops 201351168 | bytes 6602752 | tf_op jit(solution)/shard_map/dot_general | solution.py:425
  5.3 27.0 %shard_map.67 = (bf16[4,2,2,2,32,768]{5,4,3,2,1,0:T(8,128)(2,1)}, bf16[512,768]{1,0:T(8,128)(2,1)}) custom-call(bf16[32,768]{1,0:T(8,128)(2,1)} %convolution_convert_fusion.x_ref, bf16[512,4096]{1,0:T(8,128)(2,1)} %refs_0_.3, bf16[4096,768]{1,0:T(8,128)(2,1)} %refs_5_.1), custom_call_target="tpu_custom_call" | custom-call | tf_op jit(solution)/shard_map/pallas_call | solution.py:147
  32.3 0.0 copy-start
  32.3 2.7 %multiply_reduce_fusion = (f32[1024]{0:T(1024)S(1)}, f32[1024,512]{1,0:T(8,128)S(1)}) fusion(bf16[1024,768]{1,0:T(8,128)(2,1)} %bitcast.14, bf16[512,768]{1,0:T(8,128)(2,1)} %get-tuple-element.10.refs_1_), kind=kOutput, calls=%fused_computation.7 | convolution fusion | flops 806353920 | bytes 4460544 | tf_op jit(solution)/shard_map/dot_general | solution.py:428
  35.0 0.0 copy-done
  35.0 0.9 exponential_reduce_fusion
  35.9 0.6 pad_maximum_fusion.x_ref
  36.5 12.7 %shard_map.68 = f32[2,8,128]{2,1,0:T(8,128)} custom-call(f32[3,8,128]{2,1,0:T(8,128)} %pad_maximum_fusion.x_ref), custom_call_target="tpu_custom_call" | custom-call | tf_op jit(solution)/shard_map/pallas_call | solution.py:200
  49.3 0.7 bitcast_subtract_fusion
  49.9 0.7 slice_bitcast_fusion
  50.6 1.6 %fusion.3.refs_0_.refs_3_ = bf16[1024,512]{1,0:T(8,128)(2,1)} fusion(f32[1024,512]{1,0:T(8,128)S(1)} %get-tuple-element.18, f32[1024]{0:T(1024)S(1)} %slice_bitcast_fusion, s32[512]{0:T(512)S(1)} %iota_add_fusion, s32[1024]{0:T(1024)S(1)} %copy-done), kind=kLoop, calls=%fused_computation.5 | loop fusion | flops 3670016 | bytes 3155968 | tf_op jit(solution)/shard_map/convert_element_type | solution.py:439
  52.2 24.7 %shard_map.69 = (f32[32,768]{1,0:T(8,128)}, bf16[512,768]{1,0:T(8,128)(2,1)}) custom-call(bf16[1024,512]{1,0:T(8,128)(2,1)} %fusion.3.refs_0_.refs_3_, bf16[512,768]{1,0:T(8,128)(2,1)} %get-tuple-element.10.refs_1_, bf16[1024,768]{1,0:T(8,128)(2,1)} %bitcast.15, bf16[1024,512]{1,0:T(8,128)(2,1)} %fusion.3.refs_0_.refs_3_), custom_call_target="tpu_custom_call" | custom-call | tf_op jit(solution)/shard_map/pallas_call | solution.py:333
  77.0 0.6 dynamic_slice.3
  77.6 1.5 %convert_element_type.15.refs_3_.refs_4_ = bf16[32,768]{1,0:T(8,128)(2,1)} convert(f32[32,768]{1,0:T(8,128)} %get-tuple-element.12) | non-fusion elementwise | flops 24576 | bytes 147456 | tf_op jit(solution)/shard_map/convert_element_type | solution.py:452
  79.1 51.4 %shard_map.70 = (f32[128,768]{1,0:T(8,128)}, bf16[32,4096]{1,0:T(8,128)(2,1)}) custom-call(bf16[512,4096]{1,0:T(8,128)(2,1)} %refs_0_.3, bf16[512,768]{1,0:T(8,128)(2,1)} %get-tuple-element.11.refs_1_, bf16[32,4096]{1,0:T(8,128)(2,1)} %refs_2_.1, bf16[32,768]{1,0:T(8,128)(2,1)} %convert_element_type.15.refs_3_.refs_4_, ...), custom_call_target="tpu_custom_call" | custom-call | tf_op jit(solution)/shard_map/pallas_call | solution.py:333
  130.5 1.8 %copy.11 = f32[128,768]{1,0:T(8,128)} copy(f32[128,768]{1,0:T(8,128)} %get-tuple-element.22) | data formatting | bytes 786432
  132.2 1.7 %copy.12 = bf16[32,4096]{1,0:T(8,128)(2,1)} copy(bf16[32,4096]{1,0:T(8,128)(2,1)} %get-tuple-element.23) | data formatting | bytes 524288
  (1 shorter events, 0.0 us)
Async XLA Ops:
  32.3 2.7 %copy-start = (s32[1024]{0:T(1024)S(1)}, s32[1024]{0:T(1024)}, u32[]{:S(2)}) copy-start(s32[1024]{0:T(1024)} %param.7) | copy-start | bytes 12292

commit v4 on v2

--- a/solution.py
+++ b/solution.py
@@ -213,6 +213,8 @@
 def reduce_kernel(grid, orders, table, produce, beside, n_in, n_extra, *refs):
     ins, extra = refs[:n_in], refs[n_in : n_in + n_extra]
     refs = refs[n_in + n_extra :]
+    if beside is None:
+        refs = (refs[0], None) + tuple(refs[1:])
     out_ref, beside_ref, total, core_out, core_in = refs[:5]
     core_send, core_recv, send_sem, recv_sem = refs[5:9]
     outgoing, incoming = refs[9 : 9 + len(table)], refs[9 + len(table) :]
@@ -302,7 +304,8 @@
         if turn:
             core_finish(turn - 1)
     core_finish(n_row - 1)
-    beside(*extra, beside_ref)
+    if beside is not None:
+        beside(*extra, beside_ref)
     steps = core
     turns = []
     for part in range(len(orders)):
@@ -335,16 +338,16 @@
                 buffers.append(pltpu.VMEM(left + (last - first, cols), jnp.bfloat16))
     sizes = tuple(grid.sizes)
     half = pltpu.VMEM(sizes[:-1] + (rows, cols), jnp.bfloat16)
+    shapes = [jax.ShapeDtypeStruct((rows, cols), jnp.float32)]
+    if beside is not None:
+        shapes.append(jax.ShapeDtypeStruct(beside_shape, jnp.bfloat16))
     return pl.pallas_call(
         functools.partial(
             reduce_kernel, grid, orders, table, produce, beside, len(ins), len(extra)
         ),
-        out_shape=(
-            jax.ShapeDtypeStruct((rows, cols), jnp.float32),
-            jax.ShapeDtypeStruct(beside_shape, jnp.bfloat16),
-        ),
+        out_shape=shapes,
         in_specs=[pl.BlockSpec(memory_space=pltpu.VMEM)] * (len(ins) + len(extra)),
-        out_specs=[pl.BlockSpec(memory_space=pltpu.VMEM)] * 2,
+        out_specs=[pl.BlockSpec(memory_space=pltpu.VMEM)] * len(shapes),
         scratch_shapes=[
             pltpu.VMEM(sizes + (rows, cols), jnp.float32),
             half,
@@ -378,8 +381,9 @@
 
 def adapter_slab(z, width, passages_ref, dpa_ref, queries_ref, dqa_ref):
     columns = pl.ds(pl.multiple_of(z * width, width), width)
-    return contract_first(passages_ref[:, columns], dpa_ref[...]) + contract_first(
-        queries_ref[:, columns], dqa_ref[...]
+    return contract_first(
+        jnp.concatenate([passages_ref[:, columns], queries_ref[:, columns]], axis=0),
+        jnp.concatenate([dpa_ref[...], dqa_ref[...]], axis=0),
     )
 
 
@@ -401,20 +405,6 @@
     def _(step):
         rows = pl.ds(pl.multiple_of(step * block, block), block)
         dpa_ref[rows, :] = contract_first(dscores_ref[:, rows], qa_ref[...]).astype(jnp.bfloat16)
-
-
-def query_back(dqa_ref, adapter_ref, grad_ref):
-    block = min(512, grad_ref.shape[1])
-
-    @pl.loop(0, grad_ref.shape[1] // block)
-    def _(step):
-        columns = pl.ds(pl.multiple_of(step * block, block), block)
-        grad_ref[:, columns] = lax.dot_general(
-            dqa_ref[...],
-            adapter_ref[columns, :],
-            (((1,), (1,)), ((), ())),
-            preferred_element_type=jnp.float32,
-        ).astype(jnp.bfloat16)
 
 
 def thirds(rows):
@@ -469,13 +459,16 @@
         2,
     )
     dqa_own = dqa_own.astype(jnp.bfloat16)
-    adapter_grad, query_grad = reduce_scatter(
+    query_grad = lax.dot_general(
+        dqa_own, adapter, (((1,), (1,)), ((), ())), preferred_element_type=jnp.float32
+    ).astype(jnp.bfloat16)
+    (adapter_grad,) = reduce_scatter(
         grid,
         lambda z, *refs: adapter_slab(z, width // grid.n_row, *refs),
         (passages, dpa, queries, dqa_own),
-        query_back,
-        (dqa_own, adapter),
-        (own_rows, width),
+        None,
+        (),
+        None,
         width // n,
         emb,
         thirds(width // n),

time: 133 us -> 131 us (0.985)
  local copies, waits for them, and re-layouts: 4.71 us -> 2.04 us
  matrix products: 7.33 us -> 9.97 us
  Pallas kernels: 115 us -> 113 us
    unnamed x4 -> x11, local copies, waits for them, and re-layouts: 3.44 us -> 0.77 us
    dot_general x0 -> x1, matrix products: none -> 2.64 us  [per_device(): lax.dot_general(dqa_own, adapter, (((1,), (1,)), ((), ())), preferred_ele...]
    pallas_call x2, Pallas kernels: 74.8 us -> 73.1 us  [reduce_scatter(): pl.pallas_call(functools.partial(reduce_kernel, grid, orders, table, prod...]
where the time goes in v4:
time: 131 us
  Pallas kernels  113 us (86%)
  matrix products  9.97 us (8%)
  other arithmetic  5.29 us (4%)
  local copies, waits for them, and re-layouts  2.04 us (2%)
    pallas_call x2, Pallas kernels, reduce_scatter(): pl.pallas_call(functools.partial(reduce_kernel, grid, orders, table, prod...  73.1 us
    pallas_call x1, Pallas kernels, gather(): pl.pallas_call(functools.partial(gather_kernel, grid, orders, table, besi...  27.3 us
    pallas_call x1, Pallas kernels, combine_stats(): pl.pallas_call(functools.partial(stats_kernel, grid, dims), out_shape=jax...  12.5 us
    dot_general x1, matrix products, per_device(): jnp.dot(queries, adapter, preferred_element_type=jnp.float32)  4.64 us
    dot_general x1, matrix products, per_device(): lax.dot_general(qa, pa, (((1,), (1,)), ((), ())), preferred_element_type=...  2.69 us
    dot_general x1, matrix products, per_device(): lax.dot_general(dqa_own, adapter, (((1,), (1,)), ((), ())), preferred_ele...  2.64 us

profile of v4, /device:TPU:0, one launch (start us, length us, event | category | flops | bytes accessed | tf_op | source)
XLA Modules:
  0.0 130.9 jit_solution(14605120526342284700)
XLA Ops:
  0.6 4.6 %convolution_convert_fusion.1.x_ref = bf16[32,768]{1,0:T(8,128)(2,1)} fusion(bf16[32,4096]{1,0:T(8,128)(2,1)} %refs_2_.1, bf16[4096,768]{1,0:T(8,128)(2,1)} %refs_1_.1), kind=kOutput, calls=%fused_computation.9 | convolution fusion | flops 201351168 | bytes 6602752 | tf_op jit(solution)/shard_map/dot_general | solution.py:433
  5.3 27.3 %shard_map.67 = (bf16[4,2,2,2,32,768]{5,4,3,2,1,0:T(8,128)(2,1)}, bf16[512,768]{1,0:T(8,128)(2,1)}) custom-call(bf16[32,768]{1,0:T(8,128)(2,1)} %convolution_convert_fusion.1.x_ref, bf16[512,4096]{1,0:T(8,128)(2,1)} %refs_0_.3, bf16[4096,768]{1,0:T(8,128)(2,1)} %refs_1_.1), custom_call_target="tpu_custom_call" | custom-call | tf_op jit(solution)/shard_map/pallas_call | solution.py:145
  32.6 0.0 copy-start.2
  32.6 2.7 %multiply_reduce_fusion = (f32[1024]{0:T(1024)S(1)}, f32[1024,512]{1,0:T(8,128)S(1)}) fusion(bf16[1024,768]{1,0:T(8,128)(2,1)} %bitcast.18, bf16[512,768]{1,0:T(8,128)(2,1)} %get-tuple-element.8.refs_1_), kind=kOutput, calls=%fused_computation.8 | convolution fusion | flops 806353920 | bytes 4460544 | tf_op jit(solution)/shard_map/dot_general | solution.py:437
  35.3 0.0 copy-done.2
  35.3 0.9 exponential_reduce_fusion
  36.2 0.6 pad_maximum_fusion.x_ref
  36.8 12.5 %shard_map.68 = f32[2,8,128]{2,1,0:T(8,128)} custom-call(f32[3,8,128]{2,1,0:T(8,128)} %pad_maximum_fusion.x_ref), custom_call_target="tpu_custom_call" | custom-call | tf_op jit(solution)/shard_map/pallas_call | solution.py:198
  49.3 0.7 bitcast_subtract_fusion
  50.0 0.7 slice_bitcast_fusion
  50.7 0.0 slice-start
  50.7 1.6 %fusion.3.refs_0_.refs_3_ = bf16[1024,512]{1,0:T(8,128)(2,1)} fusion(f32[1024,512]{1,0:T(8,128)S(1)} %get-tuple-element.14, f32[1024]{0:T(1024)S(1)} %slice_bitcast_fusion, s32[512]{0:T(512)S(1)} %iota_add_fusion, s32[1024]{0:T(1024)S(1)} %copy-done.2), kind=kLoop, calls=%fused_computation.6 | loop fusion | flops 3670016 | bytes 3155968 | tf_op jit(solution)/shard_map/convert_element_type | solution.py:448
  52.3 0.0 slice-start.1
  52.3 23.7 %shard_map.69 = (f32[32,768]{1,0:T(8,128)}, bf16[512,768]{1,0:T(8,128)(2,1)}) custom-call(bf16[1024,512]{1,0:T(8,128)(2,1)} %fusion.3.refs_0_.refs_3_, bf16[512,768]{1,0:T(8,128)(2,1)} %get-tuple-element.8.refs_1_, bf16[1024,768]{1,0:T(8,128)(2,1)} %bitcast.19, bf16[1024,512]{1,0:T(8,128)(2,1)} %fusion.3.refs_0_.refs_3_), custom_call_target="tpu_custom_call" | custom-call | tf_op jit(solution)/shard_map/pallas_call | solution.py:344
  76.0 0.6 dynamic_slice.3
  76.6 1.5 %convert_element_type.18.refs_3_ = bf16[32,768]{1,0:T(8,128)(2,1)} convert(f32[32,768]{1,0:T(8,128)} %get-tuple-element.10) | non-fusion elementwise | flops 24576 | bytes 147456 | tf_op jit(solution)/shard_map/convert_element_type | solution.py:461
  78.1 0.0 copy-start.1
  78.1 49.4 %shard_map.70 = f32[128,768]{1,0:T(8,128)} custom-call(bf16[512,4096]{1,0:T(8,128)(2,1)} %refs_0_.3, bf16[512,768]{1,0:T(8,128)(2,1)} %get-tuple-element.9.refs_1_, bf16[32,4096]{1,0:T(8,128)(2,1)} %refs_2_.1, bf16[32,768]{1,0:T(8,128)(2,1)} %convert_element_type.18.refs_3_), custom_call_target="tpu_custom_call" | custom-call | tf_op jit(solution)/shard_map/pallas_call | solution.py:344
  127.5 0.0 slice-done
  127.5 0.0 slice-done.1
  127.5 0.0 copy-done.1
  127.5 0.0 copy-start
  127.5 2.6 %convolution_convert_fusion = bf16[32,4096]{1,0:T(8,128)(2,1)} fusion(bf16[32,768]{1,0:T(8,128)(2,1)S(1)} %copy-done.1, bf16[4096,768]{1,0:T(8,128)(2,1)S(1)} %bitcast.17), kind=kOutput, calls=%fused_computation | convolution fusion | flops 201457664 | bytes 6602752 | tf_op jit(solution)/shard_map/dot_general | solution.py:462
  130.2 0.0 copy-done
  130.2 0.7 copy.10
  (2 shorter events, 0.0 us)
Async XLA Ops:
  32.6 2.7 %copy-start.2 = (s32[1024]{0:T(1024)S(1)}, s32[1024]{0:T(1024)}, u32[]{:S(2)}) copy-start(s32[1024]{0:T(1024)} %param.7) | copy-start | bytes 12292
  50.7 76.8 %slice-start = ((s8[6291456]{0:T(1024)(128)(4,1)}), s8[4194304]{0:T(1024)(128)(4,1)S(1)}, s32[]{:S(2)}) async-start(s8[6291456]{0:T(1024)(128)(4,1)} %bitcast.16), calls=%async_computation | async-start | bytes 8388608
  52.3 75.2 %slice-start.1 = ((s8[6291456]{0:T(1024)(128)(4,1)}), s8[2097152]{0:T(1024)(128)(4,1)S(1)}, s32[]{:S(2)}) async-start(s8[6291456]{0:T(1024)(128)(4,1)} %bitcast.16), calls=%async_computation.1 | async-start | bytes 4194304
  78.1 49.4 %copy-start.1 = (bf16[32,768]{1,0:T(8,128)(2,1)S(1)}, bf16[32,768]{1,0:T(8,128)(2,1)}, u32[]{:S(2)}) copy-start(bf16[32,768]{1,0:T(8,128)(2,1)} %convert_element_type.18.refs_3_) | copy-start | bytes 147460
  127.5 2.7 %copy-start = (f32[128,768]{1,0:T(8,128)S(1)}, f32[128,768]{1,0:T(8,128)}, u32[]{:S(2)}) copy-start(f32[128,768]{1,0:T(8,128)} %shard_map.70) | copy-start | bytes 1179652

commit v5 on v4

--- a/solution.py
+++ b/solution.py
@@ -77,7 +77,13 @@
 
 def gather_kernel(grid, orders, table, beside, n_extra, x_ref, *refs):
     extra, o_ref, beside_ref = refs[:n_extra], refs[n_extra], refs[n_extra + 1]
-    send_sem, recv_sem = refs[n_extra + 2 :]
+    send_sem, recv_sem, load_sem = refs[n_extra + 2 : n_extra + 5]
+    held = refs[n_extra + 5 :]
+    loads = []
+    for at in range(n_extra):
+        load = pltpu.make_async_copy(extra[at], held[at], load_sem.at[at])
+        load.start()
+        loads.append(load)
     row, col, mine = grid.place()
     greet(grid, row, col, mine)
     o_ref[tuple(mine)] = x_ref[...]
@@ -125,7 +131,9 @@
 
     for part in range(len(orders)):
         start(part, 0)
-    beside(*extra, beside_ref)
+    for load in loads:
+        load.wait()
+    beside(*held, beside_ref)
     steps = len(grid.sizes)
     for step in range(steps):
         for part in range(len(orders)):
@@ -148,9 +156,15 @@
             jax.ShapeDtypeStruct(tuple(grid.sizes) + (rows, cols), x.dtype),
             jax.ShapeDtypeStruct(beside_shape, jnp.bfloat16),
         ),
-        in_specs=[pl.BlockSpec(memory_space=pltpu.VMEM)] * (1 + len(extra)),
+        in_specs=[pl.BlockSpec(memory_space=pltpu.VMEM)]
+        + [pl.BlockSpec(memory_space=pl.ANY)] * len(extra),
         out_specs=[pl.BlockSpec(memory_space=pltpu.VMEM)] * 2,
-        scratch_shapes=[pltpu.SemaphoreType.DMA((count,)), pltpu.SemaphoreType.DMA((count,))],
+        scratch_shapes=[
+            pltpu.SemaphoreType.DMA((count,)),
+            pltpu.SemaphoreType.DMA((count,)),
+            pltpu.SemaphoreType.DMA((len(extra),)),
+        ]
+        + [pltpu.VMEM(array.shape, array.dtype) for array in extra],
         compiler_params=pltpu.CompilerParams(
             collective_id=collective_id, has_side_effects=True, vmem_limit_bytes=LIMIT
         ),

time: 131 us -> 128 us (0.977)
  Pallas kernels: 113 us -> 110 us
    pallas_call x1, Pallas kernels: 27.3 us -> 23.6 us  [gather(): pl.pallas_call(functools.partial(gather_kernel, grid, orders, table, besi...]
where the time goes in v5:
time: 128 us
  Pallas kernels  110 us (86%)
  matrix products  9.97 us (8%)
  other arithmetic  5.29 us (4%)
  local copies, waits for them, and re-layouts  2.04 us (2%)
    pallas_call x2, Pallas kernels, reduce_scatter(): pl.pallas_call(functools.partial(reduce_kernel, grid, orders, table, prod...  73.1 us
    pallas_call x1, Pallas kernels, gather(): pl.pallas_call(functools.partial(gather_kernel, grid, orders, table, besi...  23.6 us
    pallas_call x1, Pallas kernels, combine_stats(): pl.pallas_call(functools.partial(stats_kernel, grid, dims), out_shape=jax...  13.4 us
    dot_general x1, matrix products, per_device(): jnp.dot(queries, adapter, preferred_element_type=jnp.float32)  4.64 us
    dot_general x1, matrix products, per_device(): lax.dot_general(qa, pa, (((1,), (1,)), ((), ())), preferred_element_type=...  2.7 us
    dot_general x1, matrix products, per_device(): lax.dot_general(dqa_own, adapter, (((1,), (1,)), ((), ())), preferred_ele...  2.64 us

profile of v5, /device:TPU:0, one launch (start us, length us, event | category | flops | bytes accessed | tf_op | source)
XLA Modules:
  0.0 128.1 jit_solution(15853775190490716490)
XLA Ops:
  0.6 4.6 %convolution_convert_fusion.1.x_ref = bf16[32,768]{1,0:T(8,128)(2,1)} fusion(bf16[32,4096]{1,0:T(8,128)(2,1)} %refs_2_.1, bf16[4096,768]{1,0:T(8,128)(2,1)} %refs_1_.1), kind=kOutput, calls=%fused_computation.9 | convolution fusion | flops 201351168 | bytes 6602752 | tf_op jit(solution)/shard_map/dot_general | solution.py:447
  5.3 23.6 %shard_map.67 = (bf16[4,2,2,2,32,768]{5,4,3,2,1,0:T(8,128)(2,1)}, bf16[512,768]{1,0:T(8,128)(2,1)}) custom-call(bf16[32,768]{1,0:T(8,128)(2,1)} %convolution_convert_fusion.1.x_ref, bf16[512,4096]{1,0:T(8,128)(2,1)} %refs_0_.3, bf16[4096,768]{1,0:T(8,128)(2,1)} %refs_1_.1), custom_call_target="tpu_custom_call" | custom-call | tf_op jit(solution)/shard_map/pallas_call | solution.py:153
  28.9 0.0 copy-start.2
  28.9 2.7 %multiply_reduce_fusion = (f32[1024]{0:T(1024)S(1)}, f32[1024,512]{1,0:T(8,128)S(1)}) fusion(bf16[1024,768]{1,0:T(8,128)(2,1)} %bitcast.18, bf16[512,768]{1,0:T(8,128)(2,1)} %get-tuple-element.8.refs_1_), kind=kOutput, calls=%fused_computation.8 | convolution fusion | flops 806353920 | bytes 4460544 | tf_op jit(solution)/shard_map/dot_general | solution.py:451
  31.6 0.0 copy-done.2
  31.6 0.9 exponential_reduce_fusion
  32.5 0.6 pad_maximum_fusion.x_ref
  33.1 13.4 %shard_map.68 = f32[2,8,128]{2,1,0:T(8,128)} custom-call(f32[3,8,128]{2,1,0:T(8,128)} %pad_maximum_fusion.x_ref), custom_call_target="tpu_custom_call" | custom-call | tf_op jit(solution)/shard_map/pallas_call | solution.py:212
  46.5 0.7 bitcast_subtract_fusion
  47.2 0.7 slice_bitcast_fusion
  47.9 0.0 slice-start
  47.9 1.6 %fusion.3.refs_0_.refs_3_ = bf16[1024,512]{1,0:T(8,128)(2,1)} fusion(f32[1024,512]{1,0:T(8,128)S(1)} %get-tuple-element.14, f32[1024]{0:T(1024)S(1)} %slice_bitcast_fusion, s32[512]{0:T(512)S(1)} %iota_add_fusion, s32[1024]{0:T(1024)S(1)} %copy-done.2), kind=kLoop, calls=%fused_computation.6 | loop fusion | flops 3670016 | bytes 3155968 | tf_op jit(solution)/shard_map/convert_element_type | solution.py:462
  49.5 0.0 slice-start.1
  49.5 23.7 %shard_map.69 = (f32[32,768]{1,0:T(8,128)}, bf16[512,768]{1,0:T(8,128)(2,1)}) custom-call(bf16[1024,512]{1,0:T(8,128)(2,1)} %fusion.3.refs_0_.refs_3_, bf16[512,768]{1,0:T(8,128)(2,1)} %get-tuple-element.8.refs_1_, bf16[1024,768]{1,0:T(8,128)(2,1)} %bitcast.19, bf16[1024,512]{1,0:T(8,128)(2,1)} %fusion.3.refs_0_.refs_3_), custom_call_target="tpu_custom_call" | custom-call | tf_op jit(solution)/shard_map/pallas_call | solution.py:358
  73.2 0.6 dynamic_slice.3
  73.8 1.5 %convert_element_type.18.refs_3_ = bf16[32,768]{1,0:T(8,128)(2,1)} convert(f32[32,768]{1,0:T(8,128)} %get-tuple-element.10) | non-fusion elementwise | flops 24576 | bytes 147456 | tf_op jit(solution)/shard_map/convert_element_type | solution.py:475
  75.3 0.0 copy-start.1
  75.3 49.4 %shard_map.70 = f32[128,768]{1,0:T(8,128)} custom-call(bf16[512,4096]{1,0:T(8,128)(2,1)} %refs_0_.3, bf16[512,768]{1,0:T(8,128)(2,1)} %get-tuple-element.9.refs_1_, bf16[32,4096]{1,0:T(8,128)(2,1)} %refs_2_.1, bf16[32,768]{1,0:T(8,128)(2,1)} %convert_element_type.18.refs_3_), custom_call_target="tpu_custom_call" | custom-call | tf_op jit(solution)/shard_map/pallas_call | solution.py:358
  124.7 0.0 slice-done
  124.7 0.0 slice-done.1
  124.7 0.0 copy-done.1
  124.7 0.0 copy-start
  124.7 2.6 %convolution_convert_fusion = bf16[32,4096]{1,0:T(8,128)(2,1)} fusion(bf16[32,768]{1,0:T(8,128)(2,1)S(1)} %copy-done.1, bf16[4096,768]{1,0:T(8,128)(2,1)S(1)} %bitcast.17), kind=kOutput, calls=%fused_computation | convolution fusion | flops 201457664 | bytes 6602752 | tf_op jit(solution)/shard_map/dot_general | solution.py:476
  127.4 0.0 copy-done
  127.4 0.7 copy.10
  (2 shorter events, 0.0 us)
Async XLA Ops:
  28.9 2.7 %copy-start.2 = (s32[1024]{0:T(1024)S(1)}, s32[1024]{0:T(1024)}, u32[]{:S(2)}) copy-start(s32[1024]{0:T(1024)} %param.7) | copy-start | bytes 12292
  47.9 76.8 %slice-start = ((s8[6291456]{0:T(1024)(128)(4,1)}), s8[4194304]{0:T(1024)(128)(4,1)S(1)}, s32[]{:S(2)}) async-start(s8[6291456]{0:T(1024)(128)(4,1)} %bitcast.16), calls=%async_computation | async-start | bytes 8388608
  49.5 75.2 %slice-start.1 = ((s8[6291456]{0:T(1024)(128)(4,1)}), s8[2097152]{0:T(1024)(128)(4,1)S(1)}, s32[]{:S(2)}) async-start(s8[6291456]{0:T(1024)(128)(4,1)} %bitcast.16), calls=%async_computation.1 | async-start | bytes 4194304
  75.3 49.4 %copy-start.1 = (bf16[32,768]{1,0:T(8,128)(2,1)S(1)}, bf16[32,768]{1,0:T(8,128)(2,1)}, u32[]{:S(2)}) copy-start(bf16[32,768]{1,0:T(8,128)(2,1)} %convert_element_type.18.refs_3_) | copy-start | bytes 147460
  124.7 2.7 %copy-start = (f32[128,768]{1,0:T(8,128)S(1)}, f32[128,768]{1,0:T(8,128)}, u32[]{:S(2)}) copy-start(f32[128,768]{1,0:T(8,128)} %shard_map.70) | copy-start | bytes 1179652
